TPU v7x, 128 devices: a whole 4x4x4 slice. The times are simulated.
128 devices in a mesh: prompt: 8 (over x, core), resp: 16 (over z, y).
Axes of the slice: x: 4, y: 4, z: 4, core: 2. Of those that a mesh axis runs over, the one named last changes fastest.
Arguments:
- queries: bfloat16 [128, 256, 4096], P(('prompt', 'resp')), may hold values from -5 to 5
- resp_keys: bfloat16 [128, 256, 512], P(('prompt', 'resp')), may hold values from -6 to 6
- resp_values: bfloat16 [128, 256, 512], P(('prompt', 'resp')), may hold values from -6 to 6
- grad_out: bfloat16 [128, 256, 4096], P(('prompt', 'resp')), may hold values from -24 to 24
- prompt_keys: bfloat16 [8, 256, 512], P('prompt', 'resp'), may hold values from -5 to 5
- prompt_values: bfloat16 [8, 256, 512], P('prompt', 'resp'), may hold values from -6 to 6
- group_sizes: int32 [8], replicated, may hold values from 1 to 64, 128 in all
- slot_response: int32 [128], replicated, may hold values from 0 to 127, each once
- lengths: int32 [128], P(('prompt', 'resp')), may hold values from 1 to 256, as said below
Outputs:
- grad_queries: bfloat16 [128, 256, 4096], P(('prompt', 'resp'))
- grad_resp_keys: bfloat16 [128, 256, 512], P(('prompt', 'resp'))
- grad_resp_values: bfloat16 [128, 256, 512], P(('prompt', 'resp'))
- grad_prompt_keys: float32 [8, 256, 512], P('prompt', 'resp')
- grad_prompt_values: float32 [8, 256, 512], P('prompt', 'resp')
Inputs may be any that keep to these rules, and one draw needn't show every extreme that they name: `group_sizes`: group sizes sum to 128; a group may hold a single response; the largest is exactly 64. `slot_response`: each response appears in exactly one slot. `lengths`: some response block is full.
All inputs are finite; a program needn't handle non-finite values.
Results may differ from a plain program's by a relative error of at most 0.012.
Values may be sent and summed in bfloat16 or wider, within the bound.
No kernel may reach another device: no remote copies, remote signals or barrier semaphores. Data moves between devices by JAX's collectives and lax.ppermute only.
A program may use at most 128 MiB of HBM per device.

v0:
```python
import math

import jax
import jax.numpy as jnp
from jax import lax
from jax.sharding import PartitionSpec as P

KVH = 4
HD = 128
GRP = 8


def head_grads(query, key_rows, value_rows, upstream, allowed, scaling):
    scores = (
        jnp.einsum("tgh,jh->gtj", query, key_rows, preferred_element_type=jnp.float32) * scaling
    )
    scores = jnp.where(allowed[None], scores, -jnp.inf)
    row_max = jnp.max(scores, axis=-1, keepdims=True)
    unnorm = jnp.exp(scores - row_max)
    probs = unnorm / jnp.sum(unnorm, axis=-1, keepdims=True)
    probs_low = probs.astype(jnp.bfloat16)
    attended = jnp.einsum("gtj,jh->tgh", probs_low, value_rows, preferred_element_type=jnp.float32)
    row_dot = jnp.sum(upstream.astype(jnp.float32) * attended, axis=-1)
    dprob = jnp.einsum("tgh,jh->gtj", upstream, value_rows, preferred_element_type=jnp.float32)
    dscore = (probs * (dprob - jnp.transpose(row_dot)[:, :, None])).astype(jnp.bfloat16)
    grad_q = (
        jnp.einsum("gtj,jh->tgh", dscore, key_rows, preferred_element_type=jnp.float32) * scaling
    )
    grad_k = jnp.einsum("gtj,tgh->jh", dscore, query, preferred_element_type=jnp.float32) * scaling
    grad_v = jnp.einsum("gtj,tgh->jh", probs_low, upstream, preferred_element_type=jnp.float32)
    return (grad_q, grad_k, grad_v)


def attend(query, prompt_k, prompt_v, resp_k, resp_v, upstream, length):
    tok_count = query.shape[0]
    prompt_len = prompt_k.shape[0]
    scaling = 1.0 / math.sqrt(HD)
    key_rows = jnp.concatenate([prompt_k, resp_k], 0)
    value_rows = jnp.concatenate([prompt_v, resp_v], 0)
    row_ids = jnp.arange(tok_count)[:, None]
    col_ids = jnp.arange(prompt_len + tok_count)[None, :] - prompt_len
    allowed = (col_ids < 0) | (col_ids <= row_ids) & (col_ids < length)
    live_rows = jnp.arange(tok_count) < length
    upstream = jnp.where(live_rows[:, None], upstream, jnp.zeros_like(upstream))
    query_heads = query.reshape(tok_count, KVH, GRP, HD)
    upstream_heads = upstream.reshape(tok_count, KVH, GRP, HD)
    q_parts, k_parts, v_parts = ([], [], [])
    for kv_head in range(KVH):
        lower = kv_head * HD
        grad_q, grad_k, grad_v = head_grads(
            query_heads[:, kv_head],
            key_rows[:, lower : lower + HD],
            value_rows[:, lower : lower + HD],
            upstream_heads[:, kv_head],
            allowed,
            scaling,
        )
        q_parts.append(grad_q)
        k_parts.append(grad_k)
        v_parts.append(grad_v)
    grad_q = jnp.stack(q_parts, axis=1).reshape(tok_count, KVH * GRP * HD).astype(jnp.bfloat16)
    grad_k = jnp.concatenate(k_parts, axis=1)
    grad_v = jnp.concatenate(v_parts, axis=1)
    return (
        grad_q,
        grad_k[:prompt_len],
        grad_v[:prompt_len],
        grad_k[prompt_len:].astype(jnp.bfloat16),
        grad_v[prompt_len:].astype(jnp.bfloat16),
    )


def per_device(
    queries,
    resp_keys,
    resp_values,
    grad_out,
    prompt_keys,
    prompt_values,
    group_sizes,
    slot_response,
    lengths,
):
    rows_each = prompt_keys.shape[1]
    width = prompt_keys.shape[2]
    resp_count = lax.axis_size("resp")
    prompt_count = lax.axis_size("prompt")
    prompt_len = rows_each * resp_count
    group_ends = jnp.cumsum(group_sizes)
    prompt_of = jnp.sum((slot_response[:, None] >= group_ends[None, :]).astype(jnp.int32), axis=1)
    column = lax.axis_index("prompt")
    own_slot = column * resp_count + lax.axis_index("resp")
    own_prompt = prompt_of[own_slot]
    every_k, every_v = (
        lax.all_gather(
            prompt_keys.reshape(rows_each, width), ("prompt", "resp"), axis=0, tiled=True
        ),
        lax.all_gather(
            prompt_values.reshape(rows_each, width), ("prompt", "resp"), axis=0, tiled=True
        ),
    )
    own_keys = lax.dynamic_slice_in_dim(every_k, own_prompt * prompt_len, prompt_len, 0)
    own_values = lax.dynamic_slice_in_dim(every_v, own_prompt * prompt_len, prompt_len, 0)
    grad_q, key_grad, value_grad, resp_kg, resp_vg = attend(
        queries[0], own_keys, own_values, resp_keys[0], resp_values[0], grad_out[0], lengths[0]
    )
    blank = jnp.zeros((prompt_count * prompt_len, width), jnp.float32)
    term_k = lax.dynamic_update_slice_in_dim(blank, key_grad, own_prompt * prompt_len, 0)
    term_v = lax.dynamic_update_slice_in_dim(blank, value_grad, own_prompt * prompt_len, 0)
    summed_k, summed_v = (
        lax.psum_scatter(term_k, ("prompt", "resp"), scatter_dimension=0, tiled=True),
        lax.psum_scatter(term_v, ("prompt", "resp"), scatter_dimension=0, tiled=True),
    )
    owned_k = summed_k.reshape(1, rows_each, width)
    owned_v = summed_v.reshape(1, rows_each, width)
    return (grad_q[None], resp_kg[None], resp_vg[None], owned_k, owned_v)


def solution(mesh):
    in_specs = (
        P(("prompt", "resp"), None, None),
        P(("prompt", "resp"), None, None),
        P(("prompt", "resp"), None, None),
        P(("prompt", "resp"), None, None),
        P("prompt", "resp", None),
        P("prompt", "resp", None),
        P(),
        P(),
        P(("prompt", "resp")),
    )
    out_specs = (
        P(("prompt", "resp"), None, None),
        P(("prompt", "resp"), None, None),
        P(("prompt", "resp"), None, None),
        P("prompt", "resp", None),
        P("prompt", "resp", None),
    )
    return jax.shard_map(
        per_device, mesh=mesh, in_specs=in_specs, out_specs=out_specs, check_vma=False
    )
```

profile of v0, /device:TPU:0, one launch (start us, length us, event | category | flops | bytes accessed | tf_op | source)
XLA Modules:
  0.0 1468.7 jit_solution(11731468419564530180)
XLA Ops:
  12.2 3.3 copy.103
  15.5 4.5 copy.105
  20.0 4.0 copy.106
  24.2 3.2 broadcast_select_fusion
  27.4 51.3 %all-gather.5.cloned.1.call-done = bf16[1,2048,512]{2,1,0:T(8,128)(2,1)} async-done(((bf16[1,16,512]{2,1,0:T(8,128)(2,1)}), bf16[1,2048,512]{2,1,0:T(8,128)(2,1)}) %all-gather.5.cloned.1.call-update) | async-done | bytes 2097168 | tf_op jit(solution)/shard_map/all_gather | solution.py:95
  79.7 2.7 fusion.56
  82.4 2.7 fusion.55
  85.0 2.6 fusion.54
  87.7 56.7 %all-gather.7.cloned.1.call-done = bf16[1,2048,512]{2,1,0:T(8,128)(2,1)} async-done(((bf16[1,16,512]{2,1,0:T(8,128)(2,1)}), bf16[1,2048,512]{2,1,0:T(8,128)(2,1)}) %all-gather.7.cloned.1.call-update) | async-done | bytes 2097168 | tf_op jit(solution)/shard_map/all_gather | solution.py:98
  145.4 5.2 fusion.109
  150.9 1.2 copy-done.4
  154.0 1.4 copy-done.14
  156.8 1.8 fusion.110
  159.1 1.1 fusion.41
  160.9 1.3 copy-done.15
  163.1 2.0 fusion.111
  165.5 1.1 fusion.40
  169.4 1.8 fusion.108
  171.6 1.1 fusion.43
  176.6 1.2 copy.146
  177.8 2.5 broadcast_in_dim.72.clone
  181.2 2.0 convolution_bitcast_fusion.5
  183.3 2.0 convolution_bitcast_fusion.6
  185.3 2.0 convolution_bitcast_fusion.7
  187.3 1.9 convolution_bitcast_fusion.4
  189.6 2.5 broadcast_in_dim.72.clone.1
  192.9 2.2 fusion.45
  195.6 1.1 copy-done.18
  197.2 1.1 copy-done.20
  199.1 2.9 copy.148
  204.8 617.3 %reduce-scatter.3.cloned.1.call-done = f32[16,512]{1,0:T(8,128)} async-done(((f32[2048,512]{1,0:T(8,128)}), f32[16,512]{1,0:T(8,128)}) %reduce-scatter.3.cloned.1.call-update) | async-done | bytes 32784 | tf_op jit(solution)/shard_map/reduce_scatter | solution.py:111
  822.1 640.0 %reduce-scatter.5.cloned.1.call-done = f32[16,512]{1,0:T(8,128)} async-done(((f32[2048,512]{1,0:T(8,128)}), f32[16,512]{1,0:T(8,128)}) %reduce-scatter.5.cloned.1.call-update) | async-done | bytes 32784 | tf_op jit(solution)/shard_map/reduce_scatter | solution.py:112
  (85 shorter events, 25.4 us)
Async XLA Ops:
  7.2 71.5 %all-gather.5.cloned.1.call-start = ((), (), s32[]{:S(2)}) async-start(), calls=%async_computation.4 | async-start | bytes 2113536 | tf_op jit(solution)/shard_map/all_gather | solution.py:95
  7.9 136.5 %all-gather.7.cloned.1.call-start = ((), (), s32[]{:S(2)}) async-start(), calls=%async_computation.5 | async-start | bytes 2113536 | tf_op jit(solution)/shard_map/all_gather | solution.py:98
  8.7 813.5 %reduce-scatter.3.cloned.1.call-start = ((), (), s32[]{:S(2)}) async-start(), calls=%async_computation.2 | async-start | bytes 4227072 | tf_op jit(solution)/shard_map/reduce_scatter | solution.py:111
  15.4 69.6 %copy-start.6 = (bf16[1,256,4096]{1,2,0:T(8,128)(2,1)}, bf16[1,256,4096]{1,2,0:T(8,128)(2,1)S(1)}, u32[]{:S(2)}) copy-start(bf16[1,256,4096]{1,2,0:T(8,128)(2,1)S(1)} %copy.103) | copy-start | bytes 6291460
  24.2 55.4 %copy-start.5 = (bf16[1,256,512]{2,1,0:T(8,128)(2,1)S(1)}, bf16[1,256,512]{2,1,0:T(8,128)(2,1)}, u32[]{:S(2)}) copy-start(bf16[1,256,512]{2,1,0:T(8,128)(2,1)} %param.10) | copy-start | bytes 786436
  85.0 60.3 %copy-start.10 = (bf16[1,256,512]{2,1,0:T(8,128)(2,1)S(1)}, bf16[1,256,512]{2,1,0:T(8,128)(2,1)}, u32[]{:S(2)}) copy-start(bf16[1,256,512]{2,1,0:T(8,128)(2,1)} %param.11) | copy-start | bytes 786436
  150.6 1.6 copy-start.4
  153.3 2.1 copy-start.7
  153.3 3.6 copy-start.12
  154.0 1.4 copy-start.14
  159.0 1.9 copy-start
  160.2 2.9 copy-start.11
  160.9 1.3 copy-start.15
  165.5 1.8 copy-start.2
  167.3 1.4 copy-start.17
  171.6 1.8 copy-start.8
  173.5 1.3 copy-start.19
  174.8 1.0 copy-start.13
  181.2 1281.0 %reduce-scatter.5.cloned.1.call-start = ((), (), s32[]{:S(2)}) async-start(), calls=%async_computation.3 | async-start | bytes 4227072 | tf_op jit(solution)/shard_map/reduce_scatter | solution.py:112
  181.2 2.0 copy-start.1
  183.3 2.0 copy-start.3
  185.3 2.0 copy-start.9
  192.9 2.2 copy-start.16
  195.2 1.6 copy-start.18
  196.8 1.6 copy-start.20
Sparse Core Ops, SparseCore 0:
  11.0 67.6 all-gather.4
  81.7 62.6 all-gather.6
  181.3 640.7 reduce-scatter.2
  825.0 637.1 reduce-scatter.4
where the time goes:
time: 1470 us
  waiting for transfers between devices  1370 us (93%)
  local copies, waits for them, and re-layouts  37.7 us (3%)
  matrix products  30.7 us (2%)
  other arithmetic  17.8 us (1%)
  between operations  15.6 us (1%)
    reduce_scatter x1, waiting for transfers between devices, per_device(): lax.psum_scatter(term_v, ('prompt', 'resp'), scatter_dimension=0, tiled=T...  640 us
    reduce_scatter x1, waiting for transfers between devices, per_device(): lax.psum_scatter(term_k, ('prompt', 'resp'), scatter_dimension=0, tiled=T...  617 us
    all_gather x1, waiting for transfers between devices, per_device(): lax.all_gather(prompt_values.reshape(rows_each, width), ('prompt', 'resp'...  56.7 us
    all_gather x1, waiting for transfers between devices, per_device(): lax.all_gather(prompt_keys.reshape(rows_each, width), ('prompt', 'resp'),...  51.3 us
  transfers between devices with their start and end apart: 4, of which 4 were waited for; matrix products, arithmetic and copies ran while one was open for 3% of the time, Pallas kernels for 0%

commit v1 on v0

v1 whole, which is shorter than its diff:
```python
import functools
import math

import jax
import jax.numpy as jnp
from jax import lax
from jax.experimental import pallas as pl
from jax.experimental.pallas import tpu as pltpu
from jax.sharding import PartitionSpec as P

KVH = 4
HD = 128
GRP = 8
TOK = 256
HALF = 128
PL = 256
ROWS = 16
NPROMPT = 8
SCALING = 1.0 / math.sqrt(HD)
EXP2_SCALE = SCALING * math.log2(math.e)
BF16 = jnp.bfloat16
F32 = jnp.float32


def contract_last(a, b):
    return lax.dot_general(a, b, (((1,), (1,)), ((), ())), preferred_element_type=F32)


def prompt_index(sizes_ref, slot):
    found = jnp.int32(0)
    end = jnp.int32(0)
    for p in range(NPROMPT - 1):
        end = end + sizes_ref[p]
        found = found + (slot >= end).astype(jnp.int32)
    return found


def split_kernel(keys_ref, values_ref, out_ref):
    for k in range(KVH):
        out_ref[k] = keys_ref[0, :, k * HD : (k + 1) * HD]
        out_ref[KVH + k] = values_ref[0, :, k * HD : (k + 1) * HD]


def select_kernel(sizes_ref, slots_ref, blocks_ref, out_ref):
    def body(d, carry):
        out_ref[d] = blocks_ref[prompt_index(sizes_ref, slots_ref[d])]
        return carry

    lax.fori_loop(0, out_ref.shape[0], body, 0, unroll=8)


def sum_kernel(sizes_ref, slots_ref, terms_ref, out_ref):
    out_ref[...] = jnp.zeros_like(out_ref)

    def body(d, carry):
        p = prompt_index(sizes_ref, slots_ref[d])
        out_ref[p] += terms_ref[d].astype(F32)
        return carry

    lax.fori_loop(0, terms_ref.shape[0], body, 0, unroll=8)


def join_kernel(blocks_ref, keys_ref, values_ref):
    for k in range(KVH):
        keys_ref[0, :, k * HD : (k + 1) * HD] = blocks_ref[k]
        values_ref[0, :, k * HD : (k + 1) * HD] = blocks_ref[KVH + k]


def attend_kernel(
    length_ref, q_ref, do_ref, kr_ref, vr_ref, kp_ref, vp_ref,
    dq_ref, dkr_ref, dvr_ref, dp_ref, dk_acc, dv_acc,
):
    length = length_ref[0]
    keys = jnp.concatenate([kp_ref[0], kr_ref[0]], axis=0)
    values = jnp.concatenate([vp_ref[0], vr_ref[0]], axis=0)
    keys_t = jnp.transpose(keys)
    lane = lax.broadcasted_iota(jnp.int32, (1, 2 * HALF), 1) % HALF
    causal = lax.broadcasted_iota(jnp.int32, (HALF, 2 * HALF), 0) <= lane
    dk_acc[...] = jnp.zeros_like(dk_acc)
    dv_acc[...] = jnp.zeros_like(dv_acc)

    def unit(pair, upper):
        count = PL + HALF * (1 + upper)
        rows = pl.ds(upper * HALF, HALF)
        first = pl.ds(pl.multiple_of(pair * (2 * HD), 2 * HD), HD)
        second = pl.ds(pl.multiple_of(pair * (2 * HD) + HD, HD), HD)
        q = jnp.concatenate([q_ref[0, rows, first], q_ref[0, rows, second]], axis=0)
        do = jnp.concatenate([do_ref[0, rows, first], do_ref[0, rows, second]], axis=0)
        s = contract_last(keys[:count], q)
        s = jnp.concatenate(
            [s[: count - HALF], jnp.where(causal, s[count - HALF :], -1e30)], axis=0
        )
        m = jnp.max(s, axis=0, keepdims=True)
        e = jnp.exp2(s * EXP2_SCALE - m * EXP2_SCALE)
        d = contract_last(values[:count], do)
        total = jnp.sum(e, axis=0, keepdims=True)
        inv = 1.0 / total
        r = jnp.sum(e * d, axis=0, keepdims=True) * inv
        live = lane + upper * HALF < length
        p = e * jnp.where(live, inv, 0.0)
        ds = (p * (d - r)).astype(BF16)
        dv_acc[:count] += jnp.dot(p.astype(BF16), do, preferred_element_type=F32)
        dk_acc[:count] += jnp.dot(ds, q, preferred_element_type=F32)
        dq_t = jnp.dot(keys_t[:, :count], ds, preferred_element_type=F32)
        dq = (jnp.transpose(dq_t) * SCALING).astype(BF16)
        dq_ref[0, rows, first] = dq[:HALF]
        dq_ref[0, rows, second] = dq[HALF:]

    for pair in range(GRP // 2):
        unit(pair, 0)
        unit(pair, 1)
    dk = dk_acc[...] * SCALING
    dv = dv_acc[...]
    dkr_ref[0] = dk[PL:].astype(BF16)
    dvr_ref[0] = dv[PL:].astype(BF16)
    dp_ref[0, 0] = dk[:PL].astype(BF16)
    dp_ref[1, 0] = dv[:PL].astype(BF16)


def attend(queries, resp_keys, resp_values, grad_out, prompt_kv, lengths):
    wide = pl.BlockSpec((1, TOK, GRP * HD), lambda k: (0, 0, k))
    narrow = pl.BlockSpec((1, TOK, HD), lambda k: (0, 0, k))
    return pl.pallas_call(
        attend_kernel,
        grid=(KVH,),
        in_specs=[
            pl.BlockSpec(memory_space=pltpu.SMEM),
            wide,
            wide,
            narrow,
            narrow,
            pl.BlockSpec((1, PL, HD), lambda k: (k, 0, 0)),
            pl.BlockSpec((1, PL, HD), lambda k: (KVH + k, 0, 0)),
        ],
        out_specs=[
            wide,
            narrow,
            narrow,
            pl.BlockSpec((2, 1, PL, HD), lambda k: (0, k, 0, 0)),
        ],
        out_shape=[
            jax.ShapeDtypeStruct(queries.shape, BF16),
            jax.ShapeDtypeStruct(resp_keys.shape, BF16),
            jax.ShapeDtypeStruct(resp_values.shape, BF16),
            jax.ShapeDtypeStruct((2, KVH, PL, HD), BF16),
        ],
        scratch_shapes=[pltpu.VMEM((PL + TOK, HD), F32), pltpu.VMEM((PL + TOK, HD), F32)],
        compiler_params=pltpu.CompilerParams(vmem_limit_bytes=48 * 1024 * 1024),
        cost_estimate=pl.CostEstimate(
            flops=5 * 2 * 8192 * 448 * 128, bytes_accessed=8 << 20, transcendentals=8192 * 448
        ),
        name="attend",
    )(lengths, queries, grad_out, resp_keys, resp_values, prompt_kv, prompt_kv)


def in_smem():
    return pl.BlockSpec(memory_space=pltpu.SMEM)


def in_vmem():
    return pl.BlockSpec(memory_space=pltpu.VMEM)


def per_device(
    queries,
    resp_keys,
    resp_values,
    grad_out,
    prompt_keys,
    prompt_values,
    group_sizes,
    slot_response,
    lengths,
):
    slots = slot_response.shape[0]
    split = pl.pallas_call(
        split_kernel,
        in_specs=[in_vmem(), in_vmem()],
        out_specs=in_vmem(),
        out_shape=jax.ShapeDtypeStruct((2 * KVH, ROWS, HD), BF16),
        name="split",
    )(prompt_keys, prompt_values)
    every = lax.all_to_all(split, "prompt", 0, 0)
    chosen = pl.pallas_call(
        select_kernel,
        in_specs=[in_smem(), in_smem(), in_vmem()],
        out_specs=in_vmem(),
        out_shape=jax.ShapeDtypeStruct((slots, ROWS, HD), BF16),
        name="select",
    )(group_sizes, slot_response, every)
    own = lax.all_to_all(chosen, ("prompt", "resp"), 0, 0)
    grad_q, grad_rk, grad_rv, grad_p = attend(
        queries, resp_keys, resp_values, grad_out, own.reshape(2 * KVH, PL, HD), lengths
    )
    terms = lax.all_to_all(grad_p.reshape(slots, ROWS, HD), ("prompt", "resp"), 0, 0)
    sums = pl.pallas_call(
        sum_kernel,
        in_specs=[in_smem(), in_smem(), in_vmem()],
        out_specs=in_vmem(),
        out_shape=jax.ShapeDtypeStruct((NPROMPT, ROWS, HD), F32),
        name="sum_terms",
    )(group_sizes, slot_response, terms)
    owned = lax.all_to_all(sums, "prompt", 0, 0)
    grad_pk, grad_pv = pl.pallas_call(
        join_kernel,
        in_specs=[in_vmem()],
        out_specs=[in_vmem(), in_vmem()],
        out_shape=[
            jax.ShapeDtypeStruct(prompt_keys.shape, F32),
            jax.ShapeDtypeStruct(prompt_values.shape, F32),
        ],
        name="join",
    )(owned)
    return (grad_q, grad_rk, grad_rv, grad_pk, grad_pv)


def solution(mesh):
    slot = ("prompt", "resp")
    in_specs = (
        P(slot, None, None),
        P(slot, None, None),
        P(slot, None, None),
        P(slot, None, None),
        P("prompt", "resp", None),
        P("prompt", "resp", None),
        P(),
        P(),
        P(slot),
    )
    out_specs = (
        P(slot, None, None),
        P(slot, None, None),
        P(slot, None, None),
        P("prompt", "resp", None),
        P("prompt", "resp", None),
    )
    return jax.shard_map(
        per_device, mesh=mesh, in_specs=in_specs, out_specs=out_specs, check_vma=False
    )
```

time: 1470 us -> 95.9 us (0.07)
  the two profiles are of different devices: /device:TPU:0 before, /device:TPU:1 now
where the time goes in v1:
time: 95.9 us; the launch traced here: 95.3 us
  blocking collectives  38.3 us (40%)
  Pallas kernels  28.3 us (30%)
  waiting for transfers between devices  13.4 us (14%)
  starting transfers between devices  8.87 us (9%)
  local copies, waits for them, and re-layouts  5.08 us (5%)
  between operations  1.29 us (1%)
    pallas_call x1, Pallas kernels, attend(): pl.pallas_call(attend_kernel, grid=(KVH,), in_specs=[pl.BlockSpec(memory_...  19.9 us
    all_to_all x1, blocking collectives, per_device(): lax.all_to_all(grad_p.reshape(slots, ROWS, HD), ('prompt', 'resp'), 0, 0)  18.3 us
    all_to_all x1, waiting for transfers between devices, per_device(): own = lax.all_to_all(chosen, ('prompt', 'resp'), 0, 0)  13.4 us
    all_to_all x1, blocking collectives, per_device(): every = lax.all_to_all(split, 'prompt', 0, 0)  10.6 us
    all_to_all x1, blocking collectives, per_device(): owned = lax.all_to_all(sums, 'prompt', 0, 0)  9.39 us
    all_to_all x1, starting transfers between devices, per_device(): own = lax.all_to_all(chosen, ('prompt', 'resp'), 0, 0)  8.87 us
    unnamed x8, local copies, waits for them, and re-layouts  5.08 us
    pallas_call x1, Pallas kernels, per_device(): pl.pallas_call(sum_kernel, in_specs=[in_smem(), in_smem(), in_vmem()], ou...  2.86 us
  transfers between devices with their start and end apart: 1, of which 1 were waited for; matrix products, arithmetic and copies ran while one was open for 0% of the time, Pallas kernels for 0%

profile of v1, /device:TPU:1, one launch (start us, length us, event | category | flops | bytes accessed | tf_op | source)
XLA Modules:
  0.0 95.3 jit_solution(7446746851417427929)
XLA Ops:
  0.6 1.4 %split.1 = bf16[8,16,128]{2,1,0:T(8,128)(2,1)} custom-call(bf16[1,16,512]{2,1,0:T(8,128)(2,1)} %keys_ref.1, bf16[1,16,512]{2,1,0:T(8,128)(2,1)} %values_ref.1), custom_call_target="tpu_custom_call" | custom-call | tf_op jit(solution)/shard_map/split/pallas_call | solution.py:176
  2.0 10.6 %all_to_all.20.blocks_ref = bf16[8,16,128]{2,1,0:T(8,128)(2,1)} all-to-all(bf16[8,16,128]{2,1,0:T(8,128)(2,1)} %split.1), channel_id=1, replica_groups=mesh['prompt'=8,'resp'=16] {'prompt'}, dimensions={0} | all-to-all | bytes 65536 | tf_op jit(solution)/shard_map/all_to_all | solution.py:183
  12.6 2.7 %select.1 = bf16[128,16,128]{2,1,0:T(8,128)(2,1)} custom-call(s32[8]{0:T(128)} %sizes_ref.3, s32[128]{0:T(128)} %slots_ref.3, bf16[8,16,128]{2,1,0:T(8,128)(2,1)} %all_to_all.20.blocks_ref), custom_call_target="tpu_custom_call" | custom-call | tf_op jit(solution)/shard_map/select/pallas_call | solution.py:184
  15.3 8.9 %all-to-all-start.1 = ((bf16[128,16,128]{2,1,0:T(8,128)(2,1)}), bf16[128,16,128]{2,1,0:T(8,128)(2,1)S(1)}, u32[]{:S(2)}, u32[]{:S(2)}) async-start(bf16[128,16,128]{2,1,0:T(8,128)(2,1)} %select.1), calls=%async_computation.1 | async-start | bytes 1048576 | tf_op jit(solution)/shard_map/all_to_all | solution.py:191
  24.9 13.4 %all-to-all-done.1 = bf16[128,16,128]{2,1,0:T(8,128)(2,1)S(1)} async-done(((bf16[128,16,128]{2,1,0:T(8,128)(2,1)}), bf16[128,16,128]{2,1,0:T(8,128)(2,1)S(1)}, u32[]{:S(2)}, u32[]{:S(2)}) %all-to-all-start.1) | async-done | bytes 524320 | tf_op jit(solution)/shard_map/all_to_all | solution.py:191
  38.3 0.0 copy-start
  38.3 1.6 %copy-done = bf16[1,256,4096]{2,1,0:T(8,128)(2,1)S(1)} copy-done((bf16[1,256,4096]{2,1,0:T(8,128)(2,1)S(1)}, bf16[1,256,4096]{2,1,0:T(8,128)(2,1)}, u32[]{:S(2)}) %copy-start) | copy-done | bytes 2097176
  39.9 0.0 copy-start.1
  39.9 1.6 %copy-done.1 = bf16[1,256,4096]{2,1,0:T(8,128)(2,1)S(1)} copy-done((bf16[1,256,4096]{2,1,0:T(8,128)(2,1)S(1)}, bf16[1,256,4096]{2,1,0:T(8,128)(2,1)}, u32[]{:S(2)}) %copy-start.1) | copy-done | bytes 2097176
  41.5 0.0 copy-start.2
  41.5 0.9 copy-done.2
  42.4 0.0 copy-start.3
  42.4 0.9 copy-done.3
  43.4 19.9 %attend.1 = (bf16[1,256,4096]{2,1,0:T(8,128)(2,1)}, bf16[1,256,512]{2,1,0:T(8,128)(2,1)}, bf16[1,256,512]{2,1,0:T(8,128)(2,1)}, bf16[2,4,256,128]{3,2,1,0:T(8,128)(2,1)S(1)}) custom-call(s32[1]{0:T(128)S(6)} %copy.14.length_ref, bf16[1,256,4096]{2,1,0:T(8,128)(2,1)S(1)} %copy-done, bf16[1,256,4096]{2,1,0:T(8,128)(2,1)S(1)} %copy-done.1, ...), custom_call_target="tpu_custom_call" | custom-call | flops 4697620480 | bytes 8388608 | tf_op jit(solution)/shard_map/attend/pallas_call | solution.py:123
  63.3 18.3 %all_to_all.21.terms_ref = bf16[128,16,128]{2,1,0:T(8,128)(2,1)} all-to-all(bf16[128,16,128]{2,1,0:T(8,128)(2,1)S(1)} %bitcast.4), channel_id=1, replica_groups=mesh['prompt'=8,'resp'=16] {'prompt','resp'}, dimensions={0} | all-to-all | bytes 1048576 | tf_op jit(solution)/shard_map/all_to_all | solution.py:195
  81.5 2.9 %sum_terms.1 = f32[8,16,128]{2,1,0:T(8,128)} custom-call(s32[8]{0:T(128)} %sizes_ref.3, s32[128]{0:T(128)} %slots_ref.3, bf16[128,16,128]{2,1,0:T(8,128)(2,1)} %all_to_all.21.terms_ref), custom_call_target="tpu_custom_call" | custom-call | tf_op jit(solution)/shard_map/sum_terms/pallas_call | solution.py:196
  84.4 9.4 %all_to_all.22.blocks_ref = f32[8,16,128]{2,1,0:T(8,128)} all-to-all(f32[8,16,128]{2,1,0:T(8,128)} %sum_terms.1), channel_id=1, replica_groups=mesh['prompt'=8,'resp'=16] {'prompt'}, dimensions={0} | all-to-all | bytes 131072 | tf_op jit(solution)/shard_map/all_to_all | solution.py:203
  93.8 1.5 %join.1 = (f32[1,16,512]{2,1,0:T(8,128)}, f32[1,16,512]{2,1,0:T(8,128)}) custom-call(f32[8,16,128]{2,1,0:T(8,128)} %all_to_all.22.blocks_ref), custom_call_target="tpu_custom_call" | custom-call | tf_op jit(solution)/shard_map/join/pallas_call | solution.py:204
Async XLA Ops:
  15.3 23.0 %all-to-all-start.1 = ((bf16[128,16,128]{2,1,0:T(8,128)(2,1)}), bf16[128,16,128]{2,1,0:T(8,128)(2,1)S(1)}, u32[]{:S(2)}, u32[]{:S(2)}) async-start(bf16[128,16,128]{2,1,0:T(8,128)(2,1)} %select.1), calls=%async_computation.1 | async-start | bytes 1048576 | tf_op jit(solution)/shard_map/all_to_all | solution.py:191
  38.3 1.6 %copy-start = (bf16[1,256,4096]{2,1,0:T(8,128)(2,1)S(1)}, bf16[1,256,4096]{2,1,0:T(8,128)(2,1)}, u32[]{:S(2)}) copy-start(bf16[1,256,4096]{2,1,0:T(8,128)(2,1)} %q_ref.1) | copy-start | bytes 6291460
  39.9 1.6 %copy-start.1 = (bf16[1,256,4096]{2,1,0:T(8,128)(2,1)S(1)}, bf16[1,256,4096]{2,1,0:T(8,128)(2,1)}, u32[]{:S(2)}) copy-start(bf16[1,256,4096]{2,1,0:T(8,128)(2,1)} %do_ref.1) | copy-start | bytes 6291460
  41.5 0.9 copy-start.2
  42.4 0.9 copy-start.3

commit v2 on v0

v2 whole, which is shorter than its diff:
```python
import math

import jax
import jax.numpy as jnp
from jax import lax
from jax.experimental import pallas as pl
from jax.experimental.pallas import tpu as pltpu
from jax.sharding import PartitionSpec as P

KVH = 4
HD = 128
GRP = 8
TOK = 256
HALF = 128
PL = 256
ROWS = 16
KVW = KVH * HD
NPROMPT = 8
PAIRS = GRP // 2
UNITS = 2 * PAIRS
LANES = 2 * HALF
SCALING = 1.0 / math.sqrt(HD)
EXP2_SCALE = SCALING * math.log2(math.e)
BF16 = jnp.bfloat16
F32 = jnp.float32
VMEM_LIMIT = 60 * 1024 * 1024
BOTH = ("prompt", "resp")


def contract_last(a, b):
    return lax.dot_general(a, b, (((1,), (1,)), ((), ())), preferred_element_type=F32)


def matmul(a, b):
    return jnp.dot(a, b, preferred_element_type=F32)


def index_kernel(sizes_ref, slots_ref, first_ref, out_ref):
    def body(j, carry):
        slot = slots_ref[first_ref[0] + j]
        found = jnp.int32(0)
        end = jnp.int32(0)
        for p in range(NPROMPT - 1):
            end = end + sizes_ref[p]
            found = found + (slot >= end).astype(jnp.int32)
        out_ref[j] = found
        return carry

    lax.fori_loop(0, out_ref.shape[0], body, 0)


def spread_kernel(keys_ref, values_ref, out_ref):
    for i in range(NPROMPT):
        out_ref[i] = (keys_ref if i % 2 == 0 else values_ref)[0]


def select_kernel(index_ref, blocks_ref, out_ref):
    for j in range(out_ref.shape[0]):
        out_ref[j] = blocks_ref[index_ref[j]]


def sum_kernel(index_ref, terms_ref, out_ref):
    out_ref[...] = jnp.zeros_like(out_ref)
    for j in range(terms_ref.shape[0]):
        out_ref[index_ref[j]] += terms_ref[j].astype(F32)


def join_kernel(blocks_ref, keys_ref, values_ref):
    keys_ref[0] = (blocks_ref[0] + blocks_ref[2]) + (blocks_ref[4] + blocks_ref[6])
    values_ref[0] = (blocks_ref[1] + blocks_ref[3]) + (blocks_ref[5] + blocks_ref[7])


def unit_rows(ref, pair, upper):
    rows = slice(upper * HALF, (upper + 1) * HALF)
    at = pair * 2 * HD
    return jnp.concatenate(
        [ref[0, rows, at : at + HD], ref[0, rows, at + HD : at + 2 * HD]], axis=0
    )


def all_rows(ref):
    return jnp.concatenate(
        [unit_rows(ref, pair, upper) for upper in range(2) for pair in range(PAIRS)], axis=0
    )


def resp_scores(kr, q, upper):
    count = HALF * (1 + upper)
    s = contract_last(kr[:count], q)
    lane = lax.broadcasted_iota(jnp.int32, (HALF, LANES), 1) % HALF
    causal = lax.broadcasted_iota(jnp.int32, (HALF, LANES), 0) <= lane
    last = jnp.where(causal, s[count - HALF :], -1e30)
    if upper:
        return jnp.concatenate([s[:HALF], last], axis=0)
    return last


def resp_stats_kernel(q_ref, do_ref, kr_ref, vr_ref, stats_ref):
    kr = kr_ref[0]
    vr = vr_ref[0]
    for upper in range(2):
        for pair in range(PAIRS):
            q = unit_rows(q_ref, pair, upper)
            do = unit_rows(do_ref, pair, upper)
            s = resp_scores(kr, q, upper)
            d = contract_last(vr[: HALF * (1 + upper)], do)
            m = jnp.max(s, axis=0, keepdims=True)
            e = jnp.exp2(s * EXP2_SCALE - m * EXP2_SCALE)
            total = jnp.sum(e, axis=0, keepdims=True)
            weighted = jnp.sum(e * d, axis=0, keepdims=True)
            unit = upper * PAIRS + pair
            stats_ref[0, unit, 0:1] = m
            stats_ref[0, unit, 1:2] = total
            stats_ref[0, unit, 2:3] = weighted


def prompt_kernel(
    length_ref, q_ref, do_ref, kp_ref, vp_ref, stats_ref, grad_ref, ds_ref, final_ref, p_ref
):
    length = length_ref[0]
    kp = kp_ref[...]
    vp = vp_ref[...]
    lane = lax.broadcasted_iota(jnp.int32, (1, LANES), 1) % HALF
    for upper in range(2):
        for pair in range(PAIRS):
            unit = upper * PAIRS + pair
            q = unit_rows(q_ref, pair, upper)
            do = unit_rows(do_ref, pair, upper)
            s = contract_last(kp, q)
            d = contract_last(vp, do)
            resp_m = stats_ref[0, unit, 0:1]
            m = jnp.maximum(jnp.max(s, axis=0, keepdims=True), resp_m)
            e = jnp.exp2(s * EXP2_SCALE - m * EXP2_SCALE)
            fade = jnp.exp2((resp_m - m) * EXP2_SCALE)
            total = jnp.sum(e, axis=0, keepdims=True) + fade * stats_ref[0, unit, 1:2]
            weighted = jnp.sum(e * d, axis=0, keepdims=True) + fade * stats_ref[0, unit, 2:3]
            inv = 1.0 / total
            r = weighted * inv
            inv = jnp.where(lane + upper * HALF < length, inv, 0.0)
            p = e * inv
            cols = slice(unit * LANES, (unit + 1) * LANES)
            ds_ref[0, :, cols] = (p * (d - r)).astype(BF16)
            p_ref[:, cols] = p.astype(BF16)
            final_ref[0, unit, 0:1] = m
            final_ref[0, unit, 1:2] = inv
            final_ref[0, unit, 2:3] = r
    grad_ref[0] = (matmul(ds_ref[0], all_rows(q_ref)) * SCALING).astype(BF16)
    grad_ref[1] = matmul(p_ref[...], all_rows(do_ref)).astype(BF16)


def resp_kernel(*refs):
    q_ref, do_ref, kr_ref, vr_ref, kp_ref, ds_ref, final_ref = refs[:7]
    dq_ref, dkr_ref, dvr_ref, dsr_ref, p_ref = refs[-5:]
    kr = kr_ref[0]
    vr = vr_ref[0]
    keys_t = jnp.transpose(jnp.concatenate([kp_ref[...], kr], axis=0))
    for upper in range(2):
        count = HALF * (1 + upper)
        for pair in range(PAIRS):
            unit = upper * PAIRS + pair
            q = unit_rows(q_ref, pair, upper)
            do = unit_rows(do_ref, pair, upper)
            s = resp_scores(kr, q, upper)
            d = contract_last(vr[:count], do)
            m = final_ref[0, unit, 0:1]
            inv = final_ref[0, unit, 1:2]
            r = final_ref[0, unit, 2:3]
            p = jnp.exp2(s * EXP2_SCALE - m * EXP2_SCALE) * inv
            ds = (p * (d - r)).astype(BF16)
            cols = slice(unit * LANES, (unit + 1) * LANES)
            dsr_ref[:count, cols] = ds
            p_ref[:count, cols] = p.astype(BF16)
            both = jnp.concatenate([ds_ref[0, :, cols], ds], axis=0)
            dq = (jnp.transpose(matmul(keys_t[:, : PL + count], both)) * SCALING).astype(BF16)
            rows = slice(upper * HALF, (upper + 1) * HALF)
            at = pair * 2 * HD
            dq_ref[0, rows, at : at + HD] = dq[:HALF]
            dq_ref[0, rows, at + HD : at + 2 * HD] = dq[HALF:]
    for out_ref, left_ref, right_ref, scale in (
        (dkr_ref, dsr_ref, q_ref, SCALING),
        (dvr_ref, p_ref, do_ref, 1.0),
    ):
        right = all_rows(right_ref)
        split = PAIRS * LANES
        out_ref[0, :HALF] = (matmul(left_ref[:HALF], right) * scale).astype(BF16)
        out_ref[0, HALF:] = (matmul(left_ref[HALF:, split:], right[split:]) * scale).astype(BF16)


def in_smem():
    return pl.BlockSpec(memory_space=pltpu.SMEM)


def in_vmem():
    return pl.BlockSpec(memory_space=pltpu.VMEM)


def shape_of(shape, dtype):
    return jax.ShapeDtypeStruct(shape, dtype)


def params():
    return pltpu.CompilerParams(vmem_limit_bytes=VMEM_LIMIT)


def small(kernel, name, in_specs, out_spec, out_shape):
    return pl.pallas_call(
        kernel, in_specs=in_specs, out_specs=out_spec, out_shape=out_shape, name=name
    )


def cost(keys, matmuls, heads):
    rows = heads * GRP * TOK
    return pl.CostEstimate(
        flops=2 * matmuls * rows * keys * HD * 2,
        bytes_accessed=heads * (2 << 20),
        transcendentals=rows * keys,
    )


def specs(first):
    wide = pl.BlockSpec((1, TOK, GRP * HD), lambda k: (0, 0, first + k))
    narrow = pl.BlockSpec((1, TOK, HD), lambda k: (0, 0, first + k))
    prompt = pl.BlockSpec((PL, HD), lambda k: (0, first + k))
    stats = pl.BlockSpec((1, UNITS, 8, LANES), lambda k: (first + k, 0, 0, 0))
    ds = pl.BlockSpec((1, PL, UNITS * LANES), lambda k: (first + k, 0, 0))
    return wide, narrow, prompt, stats, ds


def resp_stats(queries, grad_out, resp_keys, resp_values):
    wide, narrow, _, stats, _ = specs(0)
    return pl.pallas_call(
        resp_stats_kernel,
        grid=(KVH,),
        in_specs=[wide, wide, narrow, narrow],
        out_specs=stats,
        out_shape=shape_of((KVH, UNITS, 8, LANES), F32),
        compiler_params=params(),
        cost_estimate=cost(192, 2, KVH),
        name="resp_stats",
    )(queries, grad_out, resp_keys, resp_values)


def prompt_part(lengths, queries, grad_out, own_keys, own_values, stats_in):
    wide, _, prompt, stats, ds = specs(0)
    return pl.pallas_call(
        prompt_kernel,
        grid=(KVH,),
        in_specs=[in_smem(), wide, wide, prompt, prompt, stats],
        out_specs=[pl.BlockSpec((2, PL, HD), lambda k: (0, 0, k)), ds, stats],
        out_shape=[
            shape_of((2, PL, KVW), BF16),
            shape_of((KVH, PL, UNITS * LANES), BF16),
            shape_of((KVH, UNITS, 8, LANES), F32),
        ],
        scratch_shapes=[pltpu.VMEM((PL, UNITS * LANES), BF16)],
        compiler_params=params(),
        cost_estimate=cost(256, 4, KVH),
        name="prompt_part",
    )(lengths, queries, grad_out, own_keys, own_values, stats_in)


def resp_part(first, heads, operands, earlier):
    wide, narrow, prompt, stats, ds = specs(first)
    queries, resp_keys = operands[0], operands[2]
    in_specs = [wide, wide, narrow, narrow, prompt, ds, stats]
    aliases = {}
    if earlier:
        aliases = {len(in_specs) + i: i for i in range(3)}
        in_specs = in_specs + [pl.BlockSpec(memory_space=pl.ANY)] * 3
    return pl.pallas_call(
        resp_kernel,
        grid=(heads,),
        in_specs=in_specs,
        out_specs=[wide, narrow, narrow],
        out_shape=[
            shape_of(queries.shape, BF16),
            shape_of(resp_keys.shape, BF16),
            shape_of(resp_keys.shape, BF16),
        ],
        scratch_shapes=[
            pltpu.VMEM((TOK, UNITS * LANES), BF16),
            pltpu.VMEM((TOK, UNITS * LANES), BF16),
        ],
        input_output_aliases=aliases,
        compiler_params=params(),
        cost_estimate=cost(256, 5, heads),
        name="resp_part",
    )(*operands, *earlier)


FIRST_HEADS = 3


def per_device(
    queries,
    resp_keys,
    resp_values,
    grad_out,
    prompt_keys,
    prompt_values,
    group_sizes,
    slot_response,
    lengths,
):
    planes = lax.axis_size("prompt")
    lines = lax.axis_size("resp")
    mates = 2 * lines
    groups = [[g * mates + j for j in range(mates)] for g in range(planes // 2)]
    first = (lax.axis_index("prompt") // 2 * mates).astype(jnp.int32).reshape(1)

    index = small(
        index_kernel,
        "prompt_index",
        [in_smem()] * 3,
        in_smem(),
        shape_of((mates,), jnp.int32),
    )(group_sizes, slot_response, first)
    spread = small(
        spread_kernel,
        "spread",
        [in_vmem()] * 2,
        in_vmem(),
        shape_of((NPROMPT, ROWS, KVW), BF16),
    )(prompt_keys, prompt_values)
    every = lax.all_to_all(spread, "prompt", 0, 0)
    chosen = small(
        select_kernel,
        "select",
        [in_smem(), in_vmem()],
        in_vmem(),
        shape_of((mates, ROWS, KVW), BF16),
    )(index, every)
    queries, chosen = lax.optimization_barrier((queries, chosen))
    own = lax.all_to_all(chosen, BOTH, 0, 0, axis_index_groups=groups)
    stats = resp_stats(queries, grad_out, resp_keys, resp_values)
    own = own.reshape(2, PL, KVW)
    grad_p, ds, final = prompt_part(lengths, queries, grad_out, own[0], own[1], stats)
    terms = lax.all_to_all(
        grad_p.reshape(mates, ROWS, KVW), BOTH, 0, 0, axis_index_groups=groups
    )
    operands = (queries, grad_out, resp_keys, resp_values, own[0], ds, final)
    earlier = resp_part(0, FIRST_HEADS, operands, ())
    terms, *earlier = lax.optimization_barrier((terms, *earlier))
    sums = small(
        sum_kernel,
        "sum_terms",
        [in_smem(), in_vmem()],
        in_vmem(),
        shape_of((NPROMPT, ROWS, KVW), F32),
    )(index, terms)
    sums, *earlier = lax.optimization_barrier((sums, *earlier))
    owned = lax.all_to_all(sums, "prompt", 0, 0)
    grad_q, grad_rk, grad_rv = resp_part(
        FIRST_HEADS, KVH - FIRST_HEADS, operands, tuple(earlier)
    )
    grad_pk, grad_pv = small(
        join_kernel,
        "join",
        [in_vmem()],
        [in_vmem()] * 2,
        [shape_of(prompt_keys.shape, F32), shape_of(prompt_values.shape, F32)],
    )(owned)
    return (grad_q, grad_rk, grad_rv, grad_pk, grad_pv)


def solution(mesh):
    in_specs = (
        P(BOTH, None, None),
        P(BOTH, None, None),
        P(BOTH, None, None),
        P(BOTH, None, None),
        P("prompt", "resp", None),
        P("prompt", "resp", None),
        P(),
        P(),
        P(BOTH),
    )
    out_specs = (
        P(BOTH, None, None),
        P(BOTH, None, None),
        P(BOTH, None, None),
        P("prompt", "resp", None),
        P("prompt", "resp", None),
    )
    return jax.shard_map(
        per_device, mesh=mesh, in_specs=in_specs, out_specs=out_specs, check_vma=False
    )
```

time: 1470 us -> 79.8 us (0.05)
  the two profiles are of different devices: /device:TPU:0 before, /device:TPU:1 now
where the time goes in v2:
time: 79.8 us; the launch traced here: 79.1 us
  Pallas kernels  36.8 us (46%)
  starting transfers between devices  23.9 us (30%)
  waiting for transfers between devices  14 us (18%)
  local copies, waits for them, and re-layouts  2.99 us (4%)
  between operations  1.31 us (2%)
    pallas_call x2, Pallas kernels, resp_part(): pl.pallas_call(resp_kernel, grid=(heads,), in_specs=in_specs, out_specs=[...  12.1 us
    pallas_call x1, Pallas kernels, prompt_part(): pl.pallas_call(prompt_kernel, grid=(KVH,), in_specs=[in_smem(), wide, wid...  10.8 us
    all_to_all x1, starting transfers between devices, per_device(): own = lax.all_to_all(chosen, BOTH, 0, 0, axis_index_groups=groups)  8.97 us
    all_to_all x1, starting transfers between devices, per_device(): every = lax.all_to_all(spread, 'prompt', 0, 0)  5.8 us
    pallas_call x1, Pallas kernels, resp_stats(): pl.pallas_call(resp_stats_kernel, grid=(KVH,), in_specs=[wide, wide, narr...  5.53 us
    all_to_all x1, waiting for transfers between devices, per_device(): own = lax.all_to_all(chosen, BOTH, 0, 0, axis_index_groups=groups)  4.93 us
    all_to_all x1, starting transfers between devices, per_device(): lax.all_to_all(grad_p.reshape(mates, ROWS, KVW), BOTH, 0, 0, axis_index_g...  4.75 us
    all_to_all x1, starting transfers between devices, per_device(): owned = lax.all_to_all(sums, 'prompt', 0, 0)  4.41 us
  transfers between devices with their start and end apart: 4, of which 4 were waited for; matrix products, arithmetic and copies ran while one was open for 0% of the time, Pallas kernels for 24%

profile of v2, /device:TPU:1, one launch (start us, length us, event | category | flops | bytes accessed | tf_op | source)
XLA Modules:
  0.0 79.1 jit_solution(9482428747073528869)
XLA Ops:
  0.6 1.4 %spread.1 = bf16[8,16,512]{2,1,0:T(8,128)(2,1)} custom-call(bf16[1,16,512]{2,1,0:T(8,128)(2,1)} %keys_ref.1, bf16[1,16,512]{2,1,0:T(8,128)(2,1)} %values_ref.1), custom_call_target="tpu_custom_call" | custom-call | tf_op jit(solution)/shard_map/spread/pallas_call | solution.py:318
  2.0 5.8 %all-to-all-start = ((bf16[8,16,512]{2,1,0:T(8,128)(2,1)}), bf16[8,16,512]{2,1,0:T(8,128)(2,1)S(1)}, u32[]{:S(2)}, u32[]{:S(2)}) async-start(bf16[8,16,512]{2,1,0:T(8,128)(2,1)} %spread.1), calls=%async_computation | async-start | bytes 262144 | tf_op jit(solution)/shard_map/all_to_all | solution.py:325
  7.8 1.7 %prompt_index.1.index_ref = s32[32]{0:T(128)} custom-call(s32[8]{0:T(128)} %sizes_ref.1, s32[128]{0:T(128)} %slots_ref.1, s32[1]{0:T(128)} %bitcast.first_ref), custom_call_target="tpu_custom_call" | custom-call | tf_op jit(solution)/shard_map/prompt_index/pallas_call | solution.py:311
  9.5 3.6 %all-to-all-done.blocks_ref = bf16[8,16,512]{2,1,0:T(8,128)(2,1)S(1)} async-done(((bf16[8,16,512]{2,1,0:T(8,128)(2,1)}), bf16[8,16,512]{2,1,0:T(8,128)(2,1)S(1)}, u32[]{:S(2)}, u32[]{:S(2)}) %all-to-all-start) | async-done | bytes 131104 | tf_op jit(solution)/shard_map/all_to_all | solution.py:325
  13.1 0.0 copy-start.2
  13.1 0.7 copy-done.2
  13.8 1.7 %select.5 = bf16[32,16,512]{2,1,0:T(8,128)(2,1)} custom-call(s32[32]{0:T(128)} %prompt_index.1.index_ref, bf16[8,16,512]{2,1,0:T(8,128)(2,1)} %copy-done.2), custom_call_target="tpu_custom_call" | custom-call | tf_op jit(solution)/shard_map/select/pallas_call | solution.py:326
  15.5 9.0 %all-to-all-start.1 = ((bf16[32,16,512]{2,1,0:T(8,128)(2,1)}), bf16[32,16,512]{2,1,0:T(8,128)(2,1)S(1)}, u32[]{:S(2)}, u32[]{:S(2)}) async-start(bf16[32,16,512]{2,1,0:T(8,128)(2,1)} %select.5), calls=%async_computation.1 | async-start | bytes 1048576 | tf_op jit(solution)/shard_map/all_to_all | solution.py:334
  25.1 5.5 %resp_stats.1.stats_ref = f32[4,8,8,256]{3,2,1,0:T(8,128)} custom-call(bf16[1,256,4096]{2,1,0:T(8,128)(2,1)} %refs_0_.1, bf16[1,256,4096]{2,1,0:T(8,128)(2,1)} %refs_1_.3, bf16[1,256,512]{2,1,0:T(8,128)(2,1)} %refs_2_.3, bf16[1,256,512]{2,1,0:T(8,128)(2,1)} %refs_3_.3), custom_call_target="tpu_custom_call" | custom-call | flops 1610612736 | bytes 8388608 | tf_op jit(solution)/shard_map/resp_stats/pallas_call | solution.py:231
  30.7 4.9 %all-to-all-done.1 = bf16[32,16,512]{2,1,0:T(8,128)(2,1)S(1)} async-done(((bf16[32,16,512]{2,1,0:T(8,128)(2,1)}), bf16[32,16,512]{2,1,0:T(8,128)(2,1)S(1)}, u32[]{:S(2)}, u32[]{:S(2)}) %all-to-all-start.1) | async-done | bytes 524320 | tf_op jit(solution)/shard_map/all_to_all | solution.py:334
  35.6 0.8 %fusion = (bf16[16,16,512]{2,1,0:T(8,128)(2,1)}, bf16[16,16,512]{2,1,0:T(8,128)(2,1)}) fusion(bf16[32,16,512]{2,1,0:T(8,128)(2,1)S(1)} %all-to-all-done.1), kind=kLoop, calls=%fused_computation | loop fusion | bytes 1048576 | tf_op jit(solution)/shard_map/slice | solution.py:337
  36.4 10.8 %prompt_part.1 = (bf16[2,256,512]{2,1,0:T(8,128)(2,1)}, bf16[4,256,2048]{2,1,0:T(8,128)(2,1)}, f32[4,8,8,256]{3,2,1,0:T(8,128)}) custom-call(s32[1]{0:T(128)S(6)} %copy.20.length_ref, bf16[1,256,4096]{2,1,0:T(8,128)(2,1)} %refs_0_.1, bf16[1,256,4096]{2,1,0:T(8,128)(2,1)} %refs_1_.3, bf16[256,512]{1,0:T(8,128)(2,1)} %bitcast.4, bf16[256,512]{1,0:T(8,128)(2,1)} %bitcast.8, ...), custom_call_target="tpu_custom_call" | custom-call | flops 4294967296 | bytes 8388608 | tf_op jit(solution)/shard_map/prompt_part/pallas_call | solution.py:245
  47.3 4.7 %all-to-all-start.2 = ((bf16[32,16,512]{2,1,0:T(8,128)(2,1)}), bf16[32,16,512]{2,1,0:T(8,128)(2,1)S(1)}, u32[]{:S(2)}, u32[]{:S(2)}) async-start(bf16[32,16,512]{2,1,0:T(8,128)(2,1)} %bitcast.7), calls=%async_computation.2 | async-start | bytes 1048576 | tf_op jit(solution)/shard_map/all_to_all | solution.py:338
  52.0 7.9 %resp_part.2 = (bf16[1,256,4096]{2,1,0:T(8,128)(2,1)}, bf16[1,256,512]{2,1,0:T(8,128)(2,1)}, bf16[1,256,512]{2,1,0:T(8,128)(2,1)}) custom-call(bf16[1,256,4096]{2,1,0:T(8,128)(2,1)} %refs_0_.1, bf16[1,256,4096]{2,1,0:T(8,128)(2,1)} %refs_1_.3, bf16[1,256,512]{2,1,0:T(8,128)(2,1)} %refs_2_.3, bf16[1,256,512]{2,1,0:T(8,128)(2,1)} %refs_3_.3, ...), custom_call_target="tpu_custom_call" | custom-call | flops 4026531840 | bytes 6291456 | tf_op jit(solution)/shard_map/resp_part/pallas_call | solution.py:270
  60.0 3.2 %all-to-all-done.2.terms_ref = bf16[32,16,512]{2,1,0:T(8,128)(2,1)S(1)} async-done(((bf16[32,16,512]{2,1,0:T(8,128)(2,1)}), bf16[32,16,512]{2,1,0:T(8,128)(2,1)S(1)}, u32[]{:S(2)}, u32[]{:S(2)}) %all-to-all-start.2) | async-done | bytes 524320 | tf_op jit(solution)/shard_map/all_to_all | solution.py:338
  63.1 0.0 copy-start
  63.1 0.8 %copy-done = bf16[32,16,512]{2,1,0:T(8,128)(2,1)} copy-done((bf16[32,16,512]{2,1,0:T(8,128)(2,1)}, bf16[32,16,512]{2,1,0:T(8,128)(2,1)S(1)}, u32[]{:S(2)}) %copy-start) | copy-done | bytes 524312
  63.9 1.9 %sum_terms.1 = f32[8,16,512]{2,1,0:T(8,128)} custom-call(s32[32]{0:T(128)} %prompt_index.1.index_ref, bf16[32,16,512]{2,1,0:T(8,128)(2,1)} %copy-done), custom_call_target="tpu_custom_call" | custom-call | tf_op jit(solution)/shard_map/sum_terms/pallas_call | solution.py:344
  65.9 4.4 %all-to-all-start.3 = ((f32[8,16,512]{2,1,0:T(8,128)}), f32[8,16,512]{2,1,0:T(8,128)S(1)}, u32[]{:S(2)}, u32[]{:S(2)}) async-start(f32[8,16,512]{2,1,0:T(8,128)} %sum_terms.1), calls=%async_computation.3 | async-start | bytes 524288 | tf_op jit(solution)/shard_map/all_to_all | solution.py:352
  70.3 4.1 %resp_part.3 = (bf16[1,256,4096]{2,1,0:T(8,128)(2,1)}, bf16[1,256,512]{2,1,0:T(8,128)(2,1)}, bf16[1,256,512]{2,1,0:T(8,128)(2,1)}) custom-call(bf16[1,256,4096]{2,1,0:T(8,128)(2,1)} %refs_0_.1, bf16[1,256,4096]{2,1,0:T(8,128)(2,1)} %refs_1_.3, bf16[1,256,512]{2,1,0:T(8,128)(2,1)} %refs_2_.3, ...), custom_call_target="tpu_custom_call", output_to_operand_aliasing={{0}: (7, {}), {1}: (8, {}), {2}: (9, {})} | custom-call | flops 1342177280 | bytes 2097152 | tf_op jit(solution)/shard_map/resp_part/pallas_call | solution.py:270
  74.4 2.4 %all-to-all-done.3.blocks_ref = f32[8,16,512]{2,1,0:T(8,128)S(1)} async-done(((f32[8,16,512]{2,1,0:T(8,128)}), f32[8,16,512]{2,1,0:T(8,128)S(1)}, u32[]{:S(2)}, u32[]{:S(2)}) %all-to-all-start.3) | async-done | bytes 262176 | tf_op jit(solution)/shard_map/all_to_all | solution.py:352
  76.8 0.0 copy-start.1
  76.8 0.7 copy-done.1
  77.5 1.6 %join.1 = (f32[1,16,512]{2,1,0:T(8,128)}, f32[1,16,512]{2,1,0:T(8,128)}) custom-call(f32[8,16,512]{2,1,0:T(8,128)} %copy-done.1), custom_call_target="tpu_custom_call" | custom-call | tf_op jit(solution)/shard_map/join/pallas_call | solution.py:356
Async XLA Ops:
  2.0 11.1 %all-to-all-start = ((bf16[8,16,512]{2,1,0:T(8,128)(2,1)}), bf16[8,16,512]{2,1,0:T(8,128)(2,1)S(1)}, u32[]{:S(2)}, u32[]{:S(2)}) async-start(bf16[8,16,512]{2,1,0:T(8,128)(2,1)} %spread.1), calls=%async_computation | async-start | bytes 262144 | tf_op jit(solution)/shard_map/all_to_all | solution.py:325
  13.1 0.7 copy-start.2
  15.5 20.1 %all-to-all-start.1 = ((bf16[32,16,512]{2,1,0:T(8,128)(2,1)}), bf16[32,16,512]{2,1,0:T(8,128)(2,1)S(1)}, u32[]{:S(2)}, u32[]{:S(2)}) async-start(bf16[32,16,512]{2,1,0:T(8,128)(2,1)} %select.5), calls=%async_computation.1 | async-start | bytes 1048576 | tf_op jit(solution)/shard_map/all_to_all | solution.py:334
  47.3 15.9 %all-to-all-start.2 = ((bf16[32,16,512]{2,1,0:T(8,128)(2,1)}), bf16[32,16,512]{2,1,0:T(8,128)(2,1)S(1)}, u32[]{:S(2)}, u32[]{:S(2)}) async-start(bf16[32,16,512]{2,1,0:T(8,128)(2,1)} %bitcast.7), calls=%async_computation.2 | async-start | bytes 1048576 | tf_op jit(solution)/shard_map/all_to_all | solution.py:338
  63.1 0.8 %copy-start = (bf16[32,16,512]{2,1,0:T(8,128)(2,1)}, bf16[32,16,512]{2,1,0:T(8,128)(2,1)S(1)}, u32[]{:S(2)}) copy-start(bf16[32,16,512]{2,1,0:T(8,128)(2,1)S(1)} %all-to-all-done.2.terms_ref) | copy-start | bytes 1572868
  65.9 10.9 %all-to-all-start.3 = ((f32[8,16,512]{2,1,0:T(8,128)}), f32[8,16,512]{2,1,0:T(8,128)S(1)}, u32[]{:S(2)}, u32[]{:S(2)}) async-start(f32[8,16,512]{2,1,0:T(8,128)} %sum_terms.1), calls=%async_computation.3 | async-start | bytes 524288 | tf_op jit(solution)/shard_map/all_to_all | solution.py:352
  76.8 0.7 copy-start.1

commit v3 on v2

v3 whole, which is shorter than its diff:
```python
import math

import jax
import jax.numpy as jnp
from jax import lax
from jax.experimental import pallas as pl
from jax.experimental.pallas import tpu as pltpu
from jax.sharding import PartitionSpec as P

KVH = 4
HD = 128
GRP = 8
HEADS = KVH * GRP
DEAD = 1e30
TOK = 256
HALF = 128
PL = 256
ROWS = 16
KVW = KVH * HD
NPROMPT = 8
PAIRS = GRP // 2
UNITS = 2 * PAIRS
LANES = 2 * HALF
SCALING = 1.0 / math.sqrt(HD)
EXP2_SCALE = SCALING * math.log2(math.e)
BF16 = jnp.bfloat16
F32 = jnp.float32
VMEM_LIMIT = 119 * 512 * 1024
SMALL_LIMIT = 4 * 1024 * 1024
PROMPT_LIMIT = 24 * 1024 * 1024
BOTH = ("prompt", "resp")


def contract_last(a, b):
    return lax.dot_general(a, b, (((1,), (1,)), ((), ())), preferred_element_type=F32)


def matmul(a, b):
    return jnp.dot(a, b, preferred_element_type=F32)


def index_kernel(sizes_ref, slots_ref, first_ref, out_ref):
    def body(j, carry):
        slot = slots_ref[first_ref[0] + j]
        found = jnp.int32(0)
        end = jnp.int32(0)
        for p in range(NPROMPT - 1):
            end = end + sizes_ref[p]
            found = found + (slot >= end).astype(jnp.int32)
        out_ref[j] = found
        return carry

    lax.fori_loop(0, out_ref.shape[0], body, 0)


def spread_kernel(keys_hbm, values_hbm, out_ref, sems):
    copies = [
        pltpu.make_async_copy(ref.at[0], out_ref.at[i], sems.at[i])
        for i, ref in enumerate((keys_hbm, values_hbm))
    ]
    for copy in copies:
        copy.start()
    for copy in copies:
        copy.wait()
    for i in range(2, NPROMPT):
        out_ref[i] = out_ref[i % 2]


def select_kernel(index_ref, blocks_ref, out_ref):
    for j in range(out_ref.shape[0]):
        out_ref[j] = blocks_ref[index_ref[j]]


def sum_kernel(index_ref, terms_ref, out_ref, acc_ref):
    acc_ref[...] = jnp.zeros_like(acc_ref)
    for j in range(terms_ref.shape[0]):
        acc_ref[index_ref[j]] += terms_ref[j].astype(F32)
    out_ref[...] = acc_ref[...].astype(BF16)


def join_kernel(blocks_ref, keys_ref, values_ref):
    for first, out_ref in ((0, keys_ref), (1, values_ref)):
        terms = [blocks_ref[i].astype(F32) for i in range(first, NPROMPT, 2)]
        out_ref[0] = (terms[0] + terms[1]) + (terms[2] + terms[3])


def unit_rows(ref, pair, upper):
    rows = slice(upper * HALF, (upper + 1) * HALF)
    at = pair * 2 * HD
    return jnp.concatenate(
        [ref[0, rows, at : at + HD], ref[0, rows, at + HD : at + 2 * HD]], axis=0
    )


def all_rows(ref):
    return jnp.concatenate(
        [unit_rows(ref, pair, upper) for upper in range(2) for pair in range(PAIRS)], axis=0
    )


def resp_scores(kr, q, upper):
    count = HALF * (1 + upper)
    s = contract_last(kr[:count], q)
    lane = lax.broadcasted_iota(jnp.int32, (HALF, LANES), 1) % HALF
    causal = lax.broadcasted_iota(jnp.int32, (HALF, LANES), 0) <= lane
    last = jnp.where(causal, s[count - HALF :], -1e30)
    if upper:
        return jnp.concatenate([s[:HALF], last], axis=0)
    return last


def resp_stats_kernel(q_ref, do_ref, kr_ref, vr_ref, stats_ref):
    kr = kr_ref[0]
    vr = vr_ref[0]
    for upper in range(2):
        for pair in range(PAIRS):
            q = unit_rows(q_ref, pair, upper)
            do = unit_rows(do_ref, pair, upper)
            s = resp_scores(kr, q, upper)
            d = contract_last(vr[: HALF * (1 + upper)], do)
            m = jnp.max(s, axis=0, keepdims=True)
            e = jnp.exp2(s * EXP2_SCALE - m * EXP2_SCALE)
            total = jnp.sum(e, axis=0, keepdims=True)
            weighted = jnp.sum(e * d, axis=0, keepdims=True)
            rows = slice(upper * HALF, (upper + 1) * HALF)
            for i, value in enumerate((m, total, weighted)):
                stats_ref[2 * pair, i : i + 1, rows] = value[:, :HALF]
                stats_ref[2 * pair + 1, i : i + 1, rows] = value[:, HALF:]


def prompt_kernel(
    length_ref, q_ref, do_ref, kp_ref, vp_ref, stats_ref,
    grad_ref, keys_ref, ds_ref, final_ref, p_ref,
):
    length = length_ref[0]
    kp = kp_ref[0]
    vp = vp_ref[0]
    lane = lax.broadcasted_iota(jnp.int32, (1, TOK), 1)
    heads = [slice(h * HD, (h + 1) * HD) for h in range(GRP)]
    for h in range(GRP):
        q = q_ref[0, :, heads[h]]
        do = do_ref[0, :, heads[h]]
        s = contract_last(kp, q)
        d = contract_last(vp, do)
        resp_m = stats_ref[h, 0:1]
        m = jnp.maximum(jnp.max(s, axis=0, keepdims=True), resp_m)
        e = jnp.exp2(s * EXP2_SCALE - m * EXP2_SCALE)
        fade = jnp.exp2((resp_m - m) * EXP2_SCALE)
        total = jnp.sum(e, axis=0, keepdims=True) + fade * stats_ref[h, 1:2]
        weighted = jnp.sum(e * d, axis=0, keepdims=True) + fade * stats_ref[h, 2:3]
        r = weighted / total
        z = jnp.where(lane < length, m * EXP2_SCALE + jnp.log2(total), DEAD)
        p = jnp.exp2(s * EXP2_SCALE - z)
        cols = slice(h * TOK, (h + 1) * TOK)
        ds_ref[:, cols] = (p * (d - r)).astype(BF16)
        p_ref[:, cols] = p.astype(BF16)
        final_ref[h, 0:1] = z
        final_ref[h, 1:2] = r
    dk = matmul(ds_ref[...], jnp.concatenate([q_ref[0, :, c] for c in heads], axis=0))
    dv = matmul(p_ref[...], jnp.concatenate([do_ref[0, :, c] for c in heads], axis=0))
    grad_ref[0] = (dk * SCALING).astype(BF16)
    grad_ref[1] = dv.astype(BF16)
    keys_ref[...] = kp


def resp_kernel(
    q_ref, do_ref, kr_ref, vr_ref, kp_ref, ds_hbm, final_ref,
    dq_ref, dkr_ref, dvr_ref, dsr_ref, p_ref, ds_ref, sems,
):
    step = pl.program_id(0)
    slot = step % 2

    def load(k):
        cols = pl.ds(pl.multiple_of(k * (GRP * TOK), GRP * TOK), GRP * TOK)
        return pltpu.make_async_copy(ds_hbm.at[:, cols], ds_ref.at[k % 2], sems.at[k % 2])

    @pl.when(step == 0)
    def _():
        load(step).start()

    @pl.when(step < KVH - 1)
    def _():
        load(step + 1).start()

    kr = kr_ref[0]
    vr = vr_ref[0]
    keys_t = jnp.transpose(jnp.concatenate([kp_ref[...], kr], axis=0))
    units = [(upper, pair) for upper in range(2) for pair in range(PAIRS)]
    for unit, (upper, pair) in enumerate(units):
        count = HALF * (1 + upper)
        rows = slice(upper * HALF, (upper + 1) * HALF)
        q = unit_rows(q_ref, pair, upper)
        do = unit_rows(do_ref, pair, upper)
        s = resp_scores(kr, q, upper)
        d = contract_last(vr[:count], do)
        z, r = (
            jnp.concatenate(
                [final_ref[h, i : i + 1, rows] for h in (2 * pair, 2 * pair + 1)], axis=1
            )
            for i in range(2)
        )
        p = jnp.exp2(s * EXP2_SCALE - z)
        cols = slice(unit * LANES, (unit + 1) * LANES)
        dsr_ref[:count, cols] = (p * (d - r)).astype(BF16)
        p_ref[:count, cols] = p.astype(BF16)
    load(step).wait()
    for unit, (upper, pair) in enumerate(units):
        count = HALF * (1 + upper)
        rows = slice(upper * HALF, (upper + 1) * HALF)
        cols = slice(unit * LANES, (unit + 1) * LANES)
        prompt_ds = jnp.concatenate(
            [
                ds_ref[slot, :, h * TOK + upper * HALF : h * TOK + (upper + 1) * HALF]
                for h in (2 * pair, 2 * pair + 1)
            ],
            axis=1,
        )
        both = jnp.concatenate([prompt_ds, dsr_ref[:count, cols]], axis=0)
        dq = (jnp.transpose(matmul(keys_t[:, : PL + count], both)) * SCALING).astype(BF16)
        at = pair * 2 * HD
        dq_ref[0, rows, at : at + HD] = dq[:HALF]
        dq_ref[0, rows, at + HD : at + 2 * HD] = dq[HALF:]
    for out_ref, left_ref, right_ref, scale in (
        (dkr_ref, dsr_ref, q_ref, SCALING),
        (dvr_ref, p_ref, do_ref, 1.0),
    ):
        right = all_rows(right_ref)
        split = PAIRS * LANES
        out_ref[0, :HALF] = (matmul(left_ref[:HALF], right) * scale).astype(BF16)
        out_ref[0, HALF:] = (matmul(left_ref[HALF:, split:], right[split:]) * scale).astype(BF16)


def in_smem():
    return pl.BlockSpec(memory_space=pltpu.SMEM)


def in_vmem():
    return pl.BlockSpec(memory_space=pltpu.VMEM)


def shape_of(shape, dtype):
    return jax.ShapeDtypeStruct(shape, dtype)


def params():
    return pltpu.CompilerParams(vmem_limit_bytes=VMEM_LIMIT)


def small(kernel, name, in_specs, out_spec, out_shape, limit=SMALL_LIMIT):
    return pl.pallas_call(
        kernel,
        in_specs=in_specs,
        out_specs=out_spec,
        out_shape=out_shape,
        compiler_params=pltpu.CompilerParams(vmem_limit_bytes=limit),
        name=name,
    )


def cost(keys, matmuls, heads):
    rows = heads * GRP * TOK
    return pl.CostEstimate(
        flops=2 * matmuls * rows * keys * HD * 2,
        bytes_accessed=heads * (2 << 20),
        transcendentals=rows * keys,
    )


def specs(first):
    wide = pl.BlockSpec((1, TOK, GRP * HD), lambda k: (0, 0, first + k))
    narrow = pl.BlockSpec((1, TOK, HD), lambda k: (0, 0, first + k))
    prompt = pl.BlockSpec((PL, HD), lambda k: (0, first + k))
    stats = pl.BlockSpec((GRP, 8, TOK), lambda k: (first + k, 0, 0))
    ds = pl.BlockSpec((PL, GRP * TOK), lambda k: (0, first + k))
    return wide, narrow, prompt, stats, ds


def resp_stats(queries, grad_out, resp_keys, resp_values):
    wide, narrow, _, stats, _ = specs(0)
    return pl.pallas_call(
        resp_stats_kernel,
        grid=(KVH,),
        in_specs=[wide, wide, narrow, narrow],
        out_specs=stats,
        out_shape=shape_of((HEADS, 8, TOK), F32),
        compiler_params=params(),
        cost_estimate=cost(192, 2, KVH),
        name="resp_stats",
    )(queries, grad_out, resp_keys, resp_values)


def prompt_part(lengths, own, queries, grad_out, stats):
    queries, grad_out, stats = (
        pltpu.with_memory_space_constraint(x, pltpu.HBM) for x in (queries, grad_out, stats)
    )
    wide = pl.BlockSpec((1, TOK, GRP * HD), lambda g: (0, 0, g))
    stat = pl.BlockSpec((GRP, 8, TOK), lambda g: (g, 0, 0))
    return pl.pallas_call(
        prompt_kernel,
        grid=(KVH,),
        in_specs=[
            in_smem(),
            wide,
            wide,
            pl.BlockSpec((1, PL, HD), lambda g: (0, 0, g)),
            pl.BlockSpec((1, PL, HD), lambda g: (1, 0, g)),
            stat,
        ],
        out_specs=[
            pl.BlockSpec((2, PL, HD), lambda g: (0, 0, g)),
            pl.BlockSpec((PL, HD), lambda g: (0, g)),
            pl.BlockSpec((PL, GRP * TOK), lambda g: (0, g)),
            stat,
        ],
        out_shape=[
            pltpu.HBM((2, PL, KVW), BF16),
            pltpu.HBM((PL, KVW), BF16),
            pltpu.HBM((PL, HEADS * TOK), BF16),
            pltpu.HBM((HEADS, 8, TOK), F32),
        ],
        scratch_shapes=[
            pltpu.VMEM((PL, GRP * TOK), BF16),
        ],
        compiler_params=pltpu.CompilerParams(vmem_limit_bytes=PROMPT_LIMIT),
        cost_estimate=cost(256, 4, KVH),
        name="prompt_part",
    )(lengths, queries, grad_out, own, own, stats)


def resp_part(queries, grad_out, resp_keys, resp_values, own_keys, ds, final):
    wide, narrow, prompt, stats, _ = specs(0)
    return pl.pallas_call(
        resp_kernel,
        grid=(KVH,),
        in_specs=[
            wide, wide, narrow, narrow, prompt, pl.BlockSpec(memory_space=pl.ANY), stats,
        ],
        out_specs=[wide, narrow, narrow],
        out_shape=[
            shape_of(queries.shape, BF16),
            shape_of(resp_keys.shape, BF16),
            shape_of(resp_keys.shape, BF16),
        ],
        scratch_shapes=[
            pltpu.VMEM((TOK, UNITS * LANES), BF16),
            pltpu.VMEM((TOK, UNITS * LANES), BF16),
            pltpu.VMEM((2, PL, GRP * TOK), BF16),
            pltpu.SemaphoreType.DMA((2,)),
        ],
        compiler_params=params(),
        cost_estimate=cost(256, 5, KVH),
        name="resp_part",
    )(queries, grad_out, resp_keys, resp_values, own_keys, ds, final)


def per_device(
    queries,
    resp_keys,
    resp_values,
    grad_out,
    prompt_keys,
    prompt_values,
    group_sizes,
    slot_response,
    lengths,
):
    planes = lax.axis_size("prompt")
    lines = lax.axis_size("resp")
    mates = 2 * lines
    groups = [[g * mates + j for j in range(mates)] for g in range(planes // 2)]
    first = (lax.axis_index("prompt") // 2 * mates).astype(jnp.int32).reshape(1)

    index = small(
        index_kernel,
        "prompt_index",
        [in_smem()] * 3,
        in_smem(),
        pltpu.SMEM((mates,), jnp.int32),
        VMEM_LIMIT,
    )(group_sizes, slot_response, first)
    spread = pl.pallas_call(
        spread_kernel,
        in_specs=[pl.BlockSpec(memory_space=pl.ANY)] * 2,
        out_specs=in_vmem(),
        out_shape=pltpu.VMEM((NPROMPT, ROWS, KVW), BF16),
        scratch_shapes=[pltpu.SemaphoreType.DMA((2,))],
        compiler_params=params(),
        name="spread",
    )(prompt_keys, prompt_values)
    every = lax.all_to_all(spread, "prompt", 0, 0)
    chosen = small(
        select_kernel,
        "select",
        [in_smem(), in_vmem()],
        in_vmem(),
        shape_of((mates, ROWS, KVW), BF16),
    )(index, every)
    queries, chosen = lax.optimization_barrier((queries, chosen))
    own = lax.all_to_all(chosen, BOTH, 0, 0, axis_index_groups=groups)
    stats = resp_stats(queries, grad_out, resp_keys, resp_values)
    own = own.reshape(2, PL, KVW)
    grad_p, own_keys, ds, final = prompt_part(lengths, own, queries, grad_out, stats)
    terms = lax.all_to_all(
        grad_p.reshape(mates, ROWS, KVW), BOTH, 0, 0, axis_index_groups=groups
    )
    grads = resp_part(queries, grad_out, resp_keys, resp_values, own_keys, ds, final)
    terms, *grads = lax.optimization_barrier((terms, *grads))
    sums = pl.pallas_call(
        sum_kernel,
        in_specs=[in_smem(), in_vmem()],
        out_specs=in_vmem(),
        out_shape=pltpu.VMEM((NPROMPT, ROWS, KVW), BF16),
        scratch_shapes=[pltpu.VMEM((NPROMPT, ROWS, KVW), F32)],
        compiler_params=pltpu.CompilerParams(vmem_limit_bytes=SMALL_LIMIT),
        name="sum_terms",
    )(index, terms)
    owned = lax.all_to_all(sums, "prompt", 0, 0)
    grad_pk, grad_pv = small(
        join_kernel,
        "join",
        [in_vmem()],
        [in_vmem()] * 2,
        [shape_of(prompt_keys.shape, F32), shape_of(prompt_values.shape, F32)],
    )(owned)
    return (*grads, grad_pk, grad_pv)


def solution(mesh):
    in_specs = (
        P(BOTH, None, None),
        P(BOTH, None, None),
        P(BOTH, None, None),
        P(BOTH, None, None),
        P("prompt", "resp", None),
        P("prompt", "resp", None),
        P(),
        P(),
        P(BOTH),
    )
    out_specs = (
        P(BOTH, None, None),
        P(BOTH, None, None),
        P(BOTH, None, None),
        P("prompt", "resp", None),
        P("prompt", "resp", None),
    )
    return jax.shard_map(
        per_device, mesh=mesh, in_specs=in_specs, out_specs=out_specs, check_vma=False
    )
```

time: 79.8 us -> 71 us (0.89)
  blocking collectives: 0 us -> 8.75 us
  Pallas kernels: 36.8 us -> 29.5 us
  starting transfers between devices: 23.9 us -> 19.5 us
  local copies, waits for them, and re-layouts: 2.99 us -> 0 us
  waiting for transfers between devices: 14 us -> 11.1 us
    all_to_all x0 -> x1, blocking collectives: none -> 8.75 us  [per_device(): owned = lax.all_to_all(sums, 'prompt', 0, 0)]
    pallas_call x5 -> x4, Pallas kernels: 17.1 us -> 11.9 us  [the longest x1 9.12 us: resp_part(): pl.pallas_call(resp_kernel, grid=(KVH,), in_specs=[wide, wide, narrow, na...]
    all_to_all x1 -> x0, starting transfers between devices: 4.41 us -> none  [per_device(): owned = lax.all_to_all(sums, 'prompt', 0, 0)]
    all_to_all x1 -> x0, waiting for transfers between devices: 2.38 us -> none  [per_device(): owned = lax.all_to_all(sums, 'prompt', 0, 0)]
    unnamed x6 -> x0, local copies, waits for them, and re-layouts: 2.15 us -> none
    all_to_all x1, waiting for transfers between devices: 3.17 us -> 1.99 us  [per_device(): lax.all_to_all(grad_p.reshape(mates, ROWS, KVW), BOTH, 0, 0, axis_index_g...]
    pallas_call x1, Pallas kernels: 1.58 us -> 0.64 us  [per_device(): small(join_kernel, 'join', [in_vmem()], [in_vmem()] * 2, [shape_of(prompt...]
    pallas_call x1, Pallas kernels: 1.74 us -> 0.83 us  [per_device(): small(select_kernel, 'select', [in_smem(), in_vmem()], in_vmem(), shape_o...]
  transfers between devices with their start and end apart: 4 -> 3, of which waited for: 4 -> 3; matrix products, arithmetic and copies ran while one was open for 0% -> 0% of each run, Pallas kernels for 24% -> 22%
where the time goes in v3:
time: 71 us; the launch traced here: 70.2 us
  Pallas kernels  29.5 us (42%)
  starting transfers between devices  19.5 us (27%)
  waiting for transfers between devices  11.1 us (16%)
  blocking collectives  8.75 us (12%)
  between operations  1.33 us (2%)
    pallas_call x1, Pallas kernels, prompt_part(): pl.pallas_call(prompt_kernel, grid=(KVH,), in_specs=[in_smem(), wide, wid...  10.7 us
    pallas_call x1, Pallas kernels, resp_part(): pl.pallas_call(resp_kernel, grid=(KVH,), in_specs=[wide, wide, narrow, na...  9.12 us
    all_to_all x1, starting transfers between devices, per_device(): own = lax.all_to_all(chosen, BOTH, 0, 0, axis_index_groups=groups)  8.97 us
    all_to_all x1, blocking collectives, per_device(): owned = lax.all_to_all(sums, 'prompt', 0, 0)  8.75 us
    all_to_all x1, starting transfers between devices, per_device(): every = lax.all_to_all(spread, 'prompt', 0, 0)  5.81 us
    pallas_call x1, Pallas kernels, resp_stats(): pl.pallas_call(resp_stats_kernel, grid=(KVH,), in_specs=[wide, wide, narr...  5.42 us
    all_to_all x1, waiting for transfers between devices, per_device(): own = lax.all_to_all(chosen, BOTH, 0, 0, axis_index_groups=groups)  5.03 us
    all_to_all x1, starting transfers between devices, per_device(): lax.all_to_all(grad_p.reshape(mates, ROWS, KVW), BOTH, 0, 0, axis_index_g...  4.74 us
  transfers between devices with their start and end apart: 3, of which 3 were waited for; matrix products, arithmetic and copies ran while one was open for 0% of the time, Pallas kernels for 22%

profile of v3, /device:TPU:1, one launch (start us, length us, event | category | flops | bytes accessed | tf_op | source)
XLA Modules:
  0.0 70.2 jit_solution(16697433290796621862)
XLA Ops:
  0.6 1.4 %spread.1 = bf16[8,16,512]{2,1,0:T(8,128)(2,1)} custom-call(bf16[1,16,512]{2,1,0:T(8,128)(2,1)} %keys_hbm.1, bf16[1,16,512]{2,1,0:T(8,128)(2,1)} %values_hbm.1), custom_call_target="tpu_custom_call" | custom-call | tf_op jit(solution)/shard_map/spread/pallas_call | solution.py:381
  2.1 5.8 %all-to-all-start = ((bf16[8,16,512]{2,1,0:T(8,128)(2,1)}), bf16[8,16,512]{2,1,0:T(8,128)(2,1)S(1)}, u32[]{:S(2)}, u32[]{:S(2)}) async-start(bf16[8,16,512]{2,1,0:T(8,128)(2,1)} %spread.1), calls=%async_computation | async-start | bytes 262144 | tf_op jit(solution)/shard_map/all_to_all | solution.py:390
  7.9 1.2 %prompt_index.1.index_ref = s32[32]{0:T(128)S(4)} custom-call(s32[8]{0:T(128)} %sizes_ref.1, s32[128]{0:T(128)} %slots_ref.1, s32[1]{0:T(128)} %bitcast.first_ref), custom_call_target="tpu_custom_call" | custom-call | tf_op jit(solution)/shard_map/prompt_index/pallas_call | solution.py:373
  9.0 4.1 %all-to-all-done.blocks_ref = bf16[8,16,512]{2,1,0:T(8,128)(2,1)S(1)} async-done(((bf16[8,16,512]{2,1,0:T(8,128)(2,1)}), bf16[8,16,512]{2,1,0:T(8,128)(2,1)S(1)}, u32[]{:S(2)}, u32[]{:S(2)}) %all-to-all-start) | async-done | bytes 131104 | tf_op jit(solution)/shard_map/all_to_all | solution.py:390
  13.1 0.8 %select.5 = bf16[32,16,512]{2,1,0:T(8,128)(2,1)} custom-call(s32[32]{0:T(128)S(4)} %prompt_index.1.index_ref, bf16[8,16,512]{2,1,0:T(8,128)(2,1)S(1)} %all-to-all-done.blocks_ref), custom_call_target="tpu_custom_call" | custom-call | tf_op jit(solution)/shard_map/select/pallas_call | solution.py:391
  14.0 9.0 %all-to-all-start.1 = ((bf16[32,16,512]{2,1,0:T(8,128)(2,1)}), bf16[32,16,512]{2,1,0:T(8,128)(2,1)S(1)}, u32[]{:S(2)}, u32[]{:S(2)}) async-start(bf16[32,16,512]{2,1,0:T(8,128)(2,1)} %select.5), calls=%async_computation.1 | async-start | bytes 1048576 | tf_op jit(solution)/shard_map/all_to_all | solution.py:399
  23.6 5.4 %resp_stats.1.stats_ref = f32[32,8,256]{2,1,0:T(8,128)} custom-call(bf16[1,256,4096]{2,1,0:T(8,128)(2,1)} %q_ref.2, bf16[1,256,4096]{2,1,0:T(8,128)(2,1)} %do_ref.5, bf16[1,256,512]{2,1,0:T(8,128)(2,1)} %kr_ref.3, bf16[1,256,512]{2,1,0:T(8,128)(2,1)} %vr_ref.3), custom_call_target="tpu_custom_call" | custom-call | flops 1610612736 | bytes 8388608 | tf_op jit(solution)/shard_map/resp_stats/pallas_call | solution.py:280
  29.0 5.0 %all-to-all-done.1 = bf16[32,16,512]{2,1,0:T(8,128)(2,1)S(1)} async-done(((bf16[32,16,512]{2,1,0:T(8,128)(2,1)}), bf16[32,16,512]{2,1,0:T(8,128)(2,1)S(1)}, u32[]{:S(2)}, u32[]{:S(2)}) %all-to-all-start.1) | async-done | bytes 524320 | tf_op jit(solution)/shard_map/all_to_all | solution.py:399
  34.0 10.7 %prompt_part.1 = (bf16[2,256,512]{2,1,0:T(8,128)(2,1)}, bf16[256,512]{1,0:T(8,128)(2,1)}, bf16[256,8192]{1,0:T(8,128)(2,1)}, f32[32,8,256]{2,1,0:T(8,128)}) custom-call(s32[1]{0:T(128)S(6)} %copy.14.length_ref, bf16[1,256,4096]{2,1,0:T(8,128)(2,1)} %q_ref.2, bf16[1,256,4096]{2,1,0:T(8,128)(2,1)} %do_ref.5, bf16[2,256,512]{2,1,0:T(8,128)(2,1)S(1)} %bitcast.3, ...), custom_call_target="tpu_custom_call" | custom-call | flops 4294967296 | bytes 8388608 | tf_op jit(solution)/shard_map/prompt_part/pallas_call | solution.py:298
  44.8 4.7 %all-to-all-start.2 = ((bf16[32,16,512]{2,1,0:T(8,128)(2,1)}), bf16[32,16,512]{2,1,0:T(8,128)(2,1)S(1)}, u32[]{:S(2)}, u32[]{:S(2)}) async-start(bf16[32,16,512]{2,1,0:T(8,128)(2,1)} %bitcast.5), calls=%async_computation.2 | async-start | bytes 1048576 | tf_op jit(solution)/shard_map/all_to_all | solution.py:403
  49.5 9.1 %resp_part.1 = (bf16[1,256,4096]{2,1,0:T(8,128)(2,1)}, bf16[1,256,512]{2,1,0:T(8,128)(2,1)}, bf16[1,256,512]{2,1,0:T(8,128)(2,1)}) custom-call(bf16[1,256,4096]{2,1,0:T(8,128)(2,1)} %q_ref.2, bf16[1,256,4096]{2,1,0:T(8,128)(2,1)} %do_ref.5, bf16[1,256,512]{2,1,0:T(8,128)(2,1)} %kr_ref.3, bf16[1,256,512]{2,1,0:T(8,128)(2,1)} %vr_ref.3, ...), custom_call_target="tpu_custom_call" | custom-call | flops 5368709120 | bytes 8388608 | tf_op jit(solution)/shard_map/resp_part/pallas_call | solution.py:332
  58.7 2.0 %all-to-all-done.2.terms_ref = bf16[32,16,512]{2,1,0:T(8,128)(2,1)S(1)} async-done(((bf16[32,16,512]{2,1,0:T(8,128)(2,1)}), bf16[32,16,512]{2,1,0:T(8,128)(2,1)S(1)}, u32[]{:S(2)}, u32[]{:S(2)}) %all-to-all-start.2) | async-done | bytes 524320 | tf_op jit(solution)/shard_map/all_to_all | solution.py:403
  60.7 0.2 sum_terms.1
  60.8 8.8 %all_to_all.20.blocks_ref = bf16[8,16,512]{2,1,0:T(8,128)(2,1)S(1)} all-to-all(bf16[8,16,512]{2,1,0:T(8,128)(2,1)S(1)} %sum_terms.1), channel_id=1, replica_groups=mesh['prompt'=8,'resp'=16] {'prompt'}, dimensions={0} | all-to-all | bytes 262144 | tf_op jit(solution)/shard_map/all_to_all | solution.py:417
  69.6 0.6 join.1
Async XLA Ops:
  2.1 11.1 %all-to-all-start = ((bf16[8,16,512]{2,1,0:T(8,128)(2,1)}), bf16[8,16,512]{2,1,0:T(8,128)(2,1)S(1)}, u32[]{:S(2)}, u32[]{:S(2)}) async-start(bf16[8,16,512]{2,1,0:T(8,128)(2,1)} %spread.1), calls=%async_computation | async-start | bytes 262144 | tf_op jit(solution)/shard_map/all_to_all | solution.py:390
  14.0 20.1 %all-to-all-start.1 = ((bf16[32,16,512]{2,1,0:T(8,128)(2,1)}), bf16[32,16,512]{2,1,0:T(8,128)(2,1)S(1)}, u32[]{:S(2)}, u32[]{:S(2)}) async-start(bf16[32,16,512]{2,1,0:T(8,128)(2,1)} %select.5), calls=%async_computation.1 | async-start | bytes 1048576 | tf_op jit(solution)/shard_map/all_to_all | solution.py:399
  44.8 15.9 %all-to-all-start.2 = ((bf16[32,16,512]{2,1,0:T(8,128)(2,1)}), bf16[32,16,512]{2,1,0:T(8,128)(2,1)S(1)}, u32[]{:S(2)}, u32[]{:S(2)}) async-start(bf16[32,16,512]{2,1,0:T(8,128)(2,1)} %bitcast.5), calls=%async_computation.2 | async-start | bytes 1048576 | tf_op jit(solution)/shard_map/all_to_all | solution.py:403

commit v4 on v3

--- a/solution.py
+++ b/solution.py
@@ -1,3 +1,4 @@
+import functools
 import math
 
 import jax
@@ -12,6 +13,8 @@
 GRP = 8
 HEADS = KVH * GRP
 DEAD = 1e30
+LINES = (14, 4, 0, 5, 7, 8, 1, 3, 6, 9, 11, 12, 2, 10, 13, 15)
+FIRST_PLANE = 4
 TOK = 256
 HALF = 128
 PL = 256
@@ -39,29 +42,38 @@
     return jnp.dot(a, b, preferred_element_type=F32)
 
 
-def index_kernel(sizes_ref, slots_ref, first_ref, out_ref):
-    def body(j, carry):
-        slot = slots_ref[first_ref[0] + j]
-        found = jnp.int32(0)
-        end = jnp.int32(0)
-        for p in range(NPROMPT - 1):
-            end = end + sizes_ref[p]
-            found = found + (slot >= end).astype(jnp.int32)
-        out_ref[j] = found
-        return carry
-
-    lax.fori_loop(0, out_ref.shape[0], body, 0)
-
-
-def spread_kernel(keys_hbm, values_hbm, out_ref, sems):
+def prepare_kernel(
+    order, turn,
+    keys_hbm, values_hbm, sizes_hbm, slots_hbm, first_ref,
+    out_ref, index_ref, sizes_ref, slots_ref, sems,
+):
     copies = [
-        pltpu.make_async_copy(ref.at[0], out_ref.at[i], sems.at[i])
-        for i, ref in enumerate((keys_hbm, values_hbm))
+        pltpu.make_async_copy(src, dst, sems.at[i])
+        for i, (src, dst) in enumerate(
+            (
+                (sizes_hbm, sizes_ref),
+                (slots_hbm, slots_ref),
+                (keys_hbm.at[0], out_ref.at[0]),
+                (values_hbm.at[0], out_ref.at[1]),
+            )
+        )
     ]
     for copy in copies:
         copy.start()
-    for copy in copies:
-        copy.wait()
+    copies[0].wait()
+    copies[1].wait()
+    ends = [sizes_ref[0]]
+    for p in range(1, NPROMPT - 1):
+        ends.append(ends[-1] + sizes_ref[p])
+    for j, member in enumerate(order):
+        slot = slots_ref[first_ref[0] + member]
+        found = jnp.int32(0)
+        for end in ends:
+            found = found + (slot >= end).astype(jnp.int32)
+        found = found + (NPROMPT - turn)
+        index_ref[j] = jnp.where(found >= NPROMPT, found - NPROMPT, found)
+    copies[2].wait()
+    copies[3].wait()
     for i in range(2, NPROMPT):
         out_ref[i] = out_ref[i % 2]
 
@@ -367,27 +379,36 @@
     planes = lax.axis_size("prompt")
     lines = lax.axis_size("resp")
     mates = 2 * lines
-    groups = [[g * mates + j for j in range(mates)] for g in range(planes // 2)]
+    slots = slot_response.shape[0]
+    order = [c * lines + b for c in range(2) for b in LINES]
+    groups = [[g * mates + j for j in order] for g in range(planes // 2)]
+    turn = FIRST_PLANE
+    column = [[(i + turn) % planes for i in range(planes)]]
     first = (lax.axis_index("prompt") // 2 * mates).astype(jnp.int32).reshape(1)
 
-    index = small(
-        index_kernel,
-        "prompt_index",
-        [in_smem()] * 3,
-        in_smem(),
-        pltpu.SMEM((mates,), jnp.int32),
-        VMEM_LIMIT,
-    )(group_sizes, slot_response, first)
-    spread = pl.pallas_call(
-        spread_kernel,
-        in_specs=[pl.BlockSpec(memory_space=pl.ANY)] * 2,
-        out_specs=in_vmem(),
-        out_shape=pltpu.VMEM((NPROMPT, ROWS, KVW), BF16),
-        scratch_shapes=[pltpu.SemaphoreType.DMA((2,))],
-        compiler_params=params(),
-        name="spread",
-    )(prompt_keys, prompt_values)
-    every = lax.all_to_all(spread, "prompt", 0, 0)
+    spread, index = pl.pallas_call(
+        functools.partial(prepare_kernel, order, turn),
+        in_specs=[pl.BlockSpec(memory_space=pl.ANY)] * 4 + [in_smem()],
+        out_specs=[in_vmem(), in_smem()],
+        out_shape=[
+            pltpu.VMEM((NPROMPT, ROWS, KVW), BF16),
+            pltpu.SMEM((mates,), jnp.int32),
+        ],
+        scratch_shapes=[
+            pltpu.SMEM((NPROMPT,), jnp.int32),
+            pltpu.SMEM((slots,), jnp.int32),
+            pltpu.SemaphoreType.DMA((4,)),
+        ],
+        compiler_params=pltpu.CompilerParams(vmem_limit_bytes=SMALL_LIMIT),
+        name="prepare",
+    )(
+        *(
+            pltpu.with_memory_space_constraint(x, pltpu.HBM)
+            for x in (prompt_keys, prompt_values, group_sizes, slot_response)
+        ),
+        first,
+    )
+    every = lax.all_to_all(spread, "prompt", 0, 0, axis_index_groups=column)
     chosen = small(
         select_kernel,
         "select",
@@ -414,7 +435,7 @@
         compiler_params=pltpu.CompilerParams(vmem_limit_bytes=SMALL_LIMIT),
         name="sum_terms",
     )(index, terms)
-    owned = lax.all_to_all(sums, "prompt", 0, 0)
+    owned = lax.all_to_all(sums, "prompt", 0, 0, axis_index_groups=column)
     grad_pk, grad_pv = small(
         join_kernel,
         "join",

time: 71 us -> 67.2 us (0.946)
  waiting for transfers between devices: 11.1 us -> 1.92 us
  blocking collectives: 8.75 us -> 16.9 us
  Pallas kernels: 29.5 us -> 27.9 us
  starting transfers between devices: 19.5 us -> 18.5 us
    all_to_all x1 -> x2, blocking collectives: 8.75 us -> 16.9 us  [the longest x1 9.11 us: per_device(): every = lax.all_to_all(spread, 'prompt', 0, 0, axis_index_groups=column)]
    all_to_all x1 -> x0, starting transfers between devices: 5.81 us -> none  [per_device(): every = lax.all_to_all(spread, 'prompt', 0, 0)]
    all_to_all x1 -> x0, waiting for transfers between devices: 4.09 us -> none  [per_device(): every = lax.all_to_all(spread, 'prompt', 0, 0)]
    all_to_all x1, waiting for transfers between devices: 5.03 us -> 1.92 us  [per_device(): own = lax.all_to_all(chosen, BOTH, 0, 0, axis_index_groups=groups)]
    all_to_all x1, starting transfers between devices: 4.74 us -> 7.61 us  [per_device(): lax.all_to_all(grad_p.reshape(mates, ROWS, KVW), BOTH, 0, 0, axis_index_g...]
    all_to_all x1, waiting for transfers between devices: 1.99 us -> 0.01 us  [per_device(): lax.all_to_all(grad_p.reshape(mates, ROWS, KVW), BOTH, 0, 0, axis_index_g...]
    all_to_all x1, starting transfers between devices: 8.97 us -> 10.9 us  [per_device(): own = lax.all_to_all(chosen, BOTH, 0, 0, axis_index_groups=groups)]
    pallas_call x2 -> x1, Pallas kernels: 2.59 us -> 1.02 us  [per_device(): pl.pallas_call(functools.partial(prepare_kernel, order, turn), in_specs=[...]
  transfers between devices with their start and end apart: 3 -> 2, of which waited for: 3 -> 1; matrix products, arithmetic and copies ran while one was open for 0% -> 0% of each run, Pallas kernels for 22% -> 22%
where the time goes in v4:
time: 67.2 us; the launch traced here: 66.6 us
  Pallas kernels  27.9 us (42%)
  starting transfers between devices  18.5 us (28%)
  blocking collectives  16.9 us (25%)
  waiting for transfers between devices  1.92 us (3%)
  between operations  1.34 us (2%)
    all_to_all x1, starting transfers between devices, per_device(): own = lax.all_to_all(chosen, BOTH, 0, 0, axis_index_groups=groups)  10.9 us
    pallas_call x1, Pallas kernels, prompt_part(): pl.pallas_call(prompt_kernel, grid=(KVH,), in_specs=[in_smem(), wide, wid...  10.7 us
    pallas_call x1, Pallas kernels, resp_part(): pl.pallas_call(resp_kernel, grid=(KVH,), in_specs=[wide, wide, narrow, na...  9.15 us
    all_to_all x1, blocking collectives, per_device(): every = lax.all_to_all(spread, 'prompt', 0, 0, axis_index_groups=column)  9.11 us
    all_to_all x1, blocking collectives, per_device(): owned = lax.all_to_all(sums, 'prompt', 0, 0, axis_index_groups=column)  7.81 us
    all_to_all x1, starting transfers between devices, per_device(): lax.all_to_all(grad_p.reshape(mates, ROWS, KVW), BOTH, 0, 0, axis_index_g...  7.61 us
    pallas_call x1, Pallas kernels, resp_stats(): pl.pallas_call(resp_stats_kernel, grid=(KVH,), in_specs=[wide, wide, narr...  5.42 us
    all_to_all x1, waiting for transfers between devices, per_device(): own = lax.all_to_all(chosen, BOTH, 0, 0, axis_index_groups=groups)  1.92 us
  transfers between devices with their start and end apart: 2, of which 1 were waited for; matrix products, arithmetic and copies ran while one was open for 0% of the time, Pallas kernels for 22%

profile of v4, /device:TPU:1, one launch (start us, length us, event | category | flops | bytes accessed | tf_op | source)
XLA Modules:
  0.0 66.6 jit_solution(17028030335104230755)
XLA Ops:
  0.6 1.0 %prepare.1 = (bf16[8,16,512]{2,1,0:T(8,128)(2,1)S(1)}, s32[32]{0:T(128)S(4)}) custom-call(bf16[1,16,512]{2,1,0:T(8,128)(2,1)} %keys_hbm.1, bf16[1,16,512]{2,1,0:T(8,128)(2,1)} %values_hbm.1, s32[8]{0:T(128)} %sizes_hbm.1, s32[128]{0:T(128)} %slots_hbm.1, s32[1]{0:T(128)} %bitcast.first_ref), custom_call_target="tpu_custom_call" | custom-call | tf_op jit(solution)/shard_map/prepare/pallas_call | solution.py:389
  1.7 9.1 %all_to_all.20.blocks_ref = bf16[8,16,512]{2,1,0:T(8,128)(2,1)S(1)} all-to-all(bf16[8,16,512]{2,1,0:T(8,128)(2,1)S(1)} %get-tuple-element.23), channel_id=1, replica_groups={{64,80,96,112,0,16,32,48},{65,81,97,113,1,17,33,49},{66,82,98,114,2,18,..., dimensions={0} | all-to-all | bytes 262144 | tf_op jit(solution)/shard_map/all_to_all | solution.py:411
  10.8 0.8 %select.5 = bf16[32,16,512]{2,1,0:T(8,128)(2,1)} custom-call(s32[32]{0:T(128)S(4)} %get-tuple-element.22.index_ref, bf16[8,16,512]{2,1,0:T(8,128)(2,1)S(1)} %all_to_all.20.blocks_ref), custom_call_target="tpu_custom_call" | custom-call | tf_op jit(solution)/shard_map/select/pallas_call | solution.py:412
  11.6 10.9 %all-to-all-start.1 = ((bf16[32,16,512]{2,1,0:T(8,128)(2,1)}), bf16[32,16,512]{2,1,0:T(8,128)(2,1)S(1)}, u32[]{:S(2)}, u32[]{:S(2)}) async-start(bf16[32,16,512]{2,1,0:T(8,128)(2,1)} %select.5), calls=%async_computation.1 | async-start | bytes 1048576 | tf_op jit(solution)/shard_map/all_to_all | solution.py:420
  23.2 5.4 %resp_stats.1.stats_ref = f32[32,8,256]{2,1,0:T(8,128)} custom-call(bf16[1,256,4096]{2,1,0:T(8,128)(2,1)} %q_ref.2, bf16[1,256,4096]{2,1,0:T(8,128)(2,1)} %do_ref.5, bf16[1,256,512]{2,1,0:T(8,128)(2,1)} %kr_ref.3, bf16[1,256,512]{2,1,0:T(8,128)(2,1)} %vr_ref.3), custom_call_target="tpu_custom_call" | custom-call | flops 1610612736 | bytes 8388608 | tf_op jit(solution)/shard_map/resp_stats/pallas_call | solution.py:292
  28.6 1.9 %all-to-all-done.1 = bf16[32,16,512]{2,1,0:T(8,128)(2,1)S(1)} async-done(((bf16[32,16,512]{2,1,0:T(8,128)(2,1)}), bf16[32,16,512]{2,1,0:T(8,128)(2,1)S(1)}, u32[]{:S(2)}, u32[]{:S(2)}) %all-to-all-start.1) | async-done | bytes 524320 | tf_op jit(solution)/shard_map/all_to_all | solution.py:420
  30.5 10.7 %prompt_part.1 = (bf16[2,256,512]{2,1,0:T(8,128)(2,1)}, bf16[256,512]{1,0:T(8,128)(2,1)}, bf16[256,8192]{1,0:T(8,128)(2,1)}, f32[32,8,256]{2,1,0:T(8,128)}) custom-call(s32[1]{0:T(128)S(6)} %copy.14.length_ref, bf16[1,256,4096]{2,1,0:T(8,128)(2,1)} %q_ref.2, bf16[1,256,4096]{2,1,0:T(8,128)(2,1)} %do_ref.5, bf16[2,256,512]{2,1,0:T(8,128)(2,1)S(1)} %bitcast.3, ...), custom_call_target="tpu_custom_call" | custom-call | flops 4294967296 | bytes 8388608 | tf_op jit(solution)/shard_map/prompt_part/pallas_call | solution.py:310
  41.2 7.6 %all-to-all-start.2 = ((bf16[32,16,512]{2,1,0:T(8,128)(2,1)}), bf16[32,16,512]{2,1,0:T(8,128)(2,1)S(1)}, u32[]{:S(2)}, u32[]{:S(2)}) async-start(bf16[32,16,512]{2,1,0:T(8,128)(2,1)} %bitcast.5), calls=%async_computation.2 | async-start | bytes 1048576 | tf_op jit(solution)/shard_map/all_to_all | solution.py:424
  48.8 9.1 %resp_part.1 = (bf16[1,256,4096]{2,1,0:T(8,128)(2,1)}, bf16[1,256,512]{2,1,0:T(8,128)(2,1)}, bf16[1,256,512]{2,1,0:T(8,128)(2,1)}) custom-call(bf16[1,256,4096]{2,1,0:T(8,128)(2,1)} %q_ref.2, bf16[1,256,4096]{2,1,0:T(8,128)(2,1)} %do_ref.5, bf16[1,256,512]{2,1,0:T(8,128)(2,1)} %kr_ref.3, bf16[1,256,512]{2,1,0:T(8,128)(2,1)} %vr_ref.3, ...), custom_call_target="tpu_custom_call" | custom-call | flops 5368709120 | bytes 8388608 | tf_op jit(solution)/shard_map/resp_part/pallas_call | solution.py:344
  58.0 0.0 all-to-all-done.2.terms_ref
  58.0 0.2 sum_terms.1
  58.2 7.8 %all_to_all.21.blocks_ref = bf16[8,16,512]{2,1,0:T(8,128)(2,1)S(1)} all-to-all(bf16[8,16,512]{2,1,0:T(8,128)(2,1)S(1)} %sum_terms.1), channel_id=1, replica_groups={{64,80,96,112,0,16,32,48},{65,81,97,113,1,17,33,49},{66,82,98,114,2,18,..., dimensions={0} | all-to-all | bytes 262144 | tf_op jit(solution)/shard_map/all_to_all | solution.py:438
  66.0 0.6 join.1
Async XLA Ops:
  11.6 18.9 %all-to-all-start.1 = ((bf16[32,16,512]{2,1,0:T(8,128)(2,1)}), bf16[32,16,512]{2,1,0:T(8,128)(2,1)S(1)}, u32[]{:S(2)}, u32[]{:S(2)}) async-start(bf16[32,16,512]{2,1,0:T(8,128)(2,1)} %select.5), calls=%async_computation.1 | async-start | bytes 1048576 | tf_op jit(solution)/shard_map/all_to_all | solution.py:420
  41.2 16.8 %all-to-all-start.2 = ((bf16[32,16,512]{2,1,0:T(8,128)(2,1)}), bf16[32,16,512]{2,1,0:T(8,128)(2,1)S(1)}, u32[]{:S(2)}, u32[]{:S(2)}) async-start(bf16[32,16,512]{2,1,0:T(8,128)(2,1)} %bitcast.5), calls=%async_computation.2 | async-start | bytes 1048576 | tf_op jit(solution)/shard_map/all_to_all | solution.py:424

commit v5 on v4

--- a/solution.py
+++ b/solution.py
@@ -53,8 +53,8 @@
             (
                 (sizes_hbm, sizes_ref),
                 (slots_hbm, slots_ref),
-                (keys_hbm.at[0], out_ref.at[0]),
-                (values_hbm.at[0], out_ref.at[1]),
+                (keys_hbm.at[0], out_ref.at[1]),
+                (values_hbm.at[0], out_ref.at[0]),
             )
         )
     ]
@@ -71,7 +71,8 @@
         for end in ends:
             found = found + (slot >= end).astype(jnp.int32)
         found = found + (NPROMPT - turn)
-        index_ref[j] = jnp.where(found >= NPROMPT, found - NPROMPT, found)
+        found = jnp.where(found >= NPROMPT, found - NPROMPT, found)
+        index_ref[j] = found + 1 - 2 * (found & 1)
     copies[2].wait()
     copies[3].wait()
     for i in range(2, NPROMPT):
@@ -91,7 +92,7 @@
 
 
 def join_kernel(blocks_ref, keys_ref, values_ref):
-    for first, out_ref in ((0, keys_ref), (1, values_ref)):
+    for first, out_ref in ((1, keys_ref), (0, values_ref)):
         terms = [blocks_ref[i].astype(F32) for i in range(first, NPROMPT, 2)]
         out_ref[0] = (terms[0] + terms[1]) + (terms[2] + terms[3])
 
@@ -170,8 +171,8 @@
         final_ref[h, 1:2] = r
     dk = matmul(ds_ref[...], jnp.concatenate([q_ref[0, :, c] for c in heads], axis=0))
     dv = matmul(p_ref[...], jnp.concatenate([do_ref[0, :, c] for c in heads], axis=0))
-    grad_ref[0] = (dk * SCALING).astype(BF16)
-    grad_ref[1] = dv.astype(BF16)
+    grad_ref[0] = dv.astype(BF16)
+    grad_ref[1] = (dk * SCALING).astype(BF16)
     keys_ref[...] = kp
 
 
@@ -314,8 +315,8 @@
             in_smem(),
             wide,
             wide,
+            pl.BlockSpec((1, PL, HD), lambda g: (1, 0, g)),
             pl.BlockSpec((1, PL, HD), lambda g: (0, 0, g)),
-            pl.BlockSpec((1, PL, HD), lambda g: (1, 0, g)),
             stat,
         ],
         out_specs=[
@@ -380,10 +381,10 @@
     lines = lax.axis_size("resp")
     mates = 2 * lines
     slots = slot_response.shape[0]
-    order = [c * lines + b for c in range(2) for b in LINES]
+    order = [c * lines + b for c in (1, 0) for b in LINES]
     groups = [[g * mates + j for j in order] for g in range(planes // 2)]
     turn = FIRST_PLANE
-    column = [[(i + turn) % planes for i in range(planes)]]
+    column = [[(i + turn) % planes ^ 1 for i in range(planes)]]
     first = (lax.axis_index("prompt") // 2 * mates).astype(jnp.int32).reshape(1)
 
     spread, index = pl.pallas_call(

time: 67.2 us -> 65.5 us (0.975)
  starting transfers between devices: 18.5 us -> 17 us
    all_to_all x1, starting transfers between devices: 10.9 us -> 9.94 us  [per_device(): own = lax.all_to_all(chosen, BOTH, 0, 0, axis_index_groups=groups)]
where the time goes in v5:
time: 65.5 us; the launch traced here: 64.9 us
  Pallas kernels  28 us (43%)
  starting transfers between devices  17 us (26%)
  blocking collectives  16.7 us (25%)
  waiting for transfers between devices  1.92 us (3%)
  between operations  1.34 us (2%)
    pallas_call x1, Pallas kernels, prompt_part(): pl.pallas_call(prompt_kernel, grid=(KVH,), in_specs=[in_smem(), wide, wid...  10.7 us
    all_to_all x1, starting transfers between devices, per_device(): own = lax.all_to_all(chosen, BOTH, 0, 0, axis_index_groups=groups)  9.94 us
    pallas_call x1, Pallas kernels, resp_part(): pl.pallas_call(resp_kernel, grid=(KVH,), in_specs=[wide, wide, narrow, na...  9.15 us
    all_to_all x1, blocking collectives, per_device(): every = lax.all_to_all(spread, 'prompt', 0, 0, axis_index_groups=column)  9.08 us
    all_to_all x1, blocking collectives, per_device(): owned = lax.all_to_all(sums, 'prompt', 0, 0, axis_index_groups=column)  7.65 us
    all_to_all x1, starting transfers between devices, per_device(): lax.all_to_all(grad_p.reshape(mates, ROWS, KVW), BOTH, 0, 0, axis_index_g...  7.03 us
    pallas_call x1, Pallas kernels, resp_stats(): pl.pallas_call(resp_stats_kernel, grid=(KVH,), in_specs=[wide, wide, narr...  5.42 us
    all_to_all x1, waiting for transfers between devices, per_device(): own = lax.all_to_all(chosen, BOTH, 0, 0, axis_index_groups=groups)  1.92 us
  transfers between devices with their start and end apart: 2, of which 1 were waited for; matrix products, arithmetic and copies ran while one was open for 0% of the time, Pallas kernels for 22%

profile of v5, /device:TPU:1, one launch (start us, length us, event | category | flops | bytes accessed | tf_op | source)
XLA Modules:
  0.0 64.9 jit_solution(2123031180661254844)
XLA Ops:
  0.6 1.1 %prepare.1 = (bf16[8,16,512]{2,1,0:T(8,128)(2,1)S(1)}, s32[32]{0:T(128)S(4)}) custom-call(bf16[1,16,512]{2,1,0:T(8,128)(2,1)} %keys_hbm.1, bf16[1,16,512]{2,1,0:T(8,128)(2,1)} %values_hbm.1, s32[8]{0:T(128)} %sizes_hbm.1, s32[128]{0:T(128)} %slots_hbm.1, s32[1]{0:T(128)} %bitcast.first_ref), custom_call_target="tpu_custom_call" | custom-call | tf_op jit(solution)/shard_map/prepare/pallas_call | solution.py:390
  1.7 9.1 %all_to_all.20.blocks_ref = bf16[8,16,512]{2,1,0:T(8,128)(2,1)S(1)} all-to-all(bf16[8,16,512]{2,1,0:T(8,128)(2,1)S(1)} %get-tuple-element.23), channel_id=1, replica_groups={{80,64,112,96,16,0,48,32},{81,65,113,97,17,1,49,33},{82,66,114,98,18,2,..., dimensions={0} | all-to-all | bytes 262144 | tf_op jit(solution)/shard_map/all_to_all | solution.py:412
  10.8 0.8 %select.5 = bf16[32,16,512]{2,1,0:T(8,128)(2,1)} custom-call(s32[32]{0:T(128)S(4)} %get-tuple-element.22.index_ref, bf16[8,16,512]{2,1,0:T(8,128)(2,1)S(1)} %all_to_all.20.blocks_ref), custom_call_target="tpu_custom_call" | custom-call | tf_op jit(solution)/shard_map/select/pallas_call | solution.py:413
  11.6 9.9 %all-to-all-start.1 = ((bf16[32,16,512]{2,1,0:T(8,128)(2,1)}), bf16[32,16,512]{2,1,0:T(8,128)(2,1)S(1)}, u32[]{:S(2)}, u32[]{:S(2)}) async-start(bf16[32,16,512]{2,1,0:T(8,128)(2,1)} %select.5), calls=%async_computation.1 | async-start | bytes 1048576 | tf_op jit(solution)/shard_map/all_to_all | solution.py:421
  22.2 5.4 %resp_stats.1.stats_ref = f32[32,8,256]{2,1,0:T(8,128)} custom-call(bf16[1,256,4096]{2,1,0:T(8,128)(2,1)} %q_ref.2, bf16[1,256,4096]{2,1,0:T(8,128)(2,1)} %do_ref.5, bf16[1,256,512]{2,1,0:T(8,128)(2,1)} %kr_ref.3, bf16[1,256,512]{2,1,0:T(8,128)(2,1)} %vr_ref.3), custom_call_target="tpu_custom_call" | custom-call | flops 1610612736 | bytes 8388608 | tf_op jit(solution)/shard_map/resp_stats/pallas_call | solution.py:293
  27.6 1.9 %all-to-all-done.1 = bf16[32,16,512]{2,1,0:T(8,128)(2,1)S(1)} async-done(((bf16[32,16,512]{2,1,0:T(8,128)(2,1)}), bf16[32,16,512]{2,1,0:T(8,128)(2,1)S(1)}, u32[]{:S(2)}, u32[]{:S(2)}) %all-to-all-start.1) | async-done | bytes 524320 | tf_op jit(solution)/shard_map/all_to_all | solution.py:421
  29.5 10.7 %prompt_part.1 = (bf16[2,256,512]{2,1,0:T(8,128)(2,1)}, bf16[256,512]{1,0:T(8,128)(2,1)}, bf16[256,8192]{1,0:T(8,128)(2,1)}, f32[32,8,256]{2,1,0:T(8,128)}) custom-call(s32[1]{0:T(128)S(6)} %copy.14.length_ref, bf16[1,256,4096]{2,1,0:T(8,128)(2,1)} %q_ref.2, bf16[1,256,4096]{2,1,0:T(8,128)(2,1)} %do_ref.5, bf16[2,256,512]{2,1,0:T(8,128)(2,1)S(1)} %bitcast.3, ...), custom_call_target="tpu_custom_call" | custom-call | flops 4294967296 | bytes 8388608 | tf_op jit(solution)/shard_map/prompt_part/pallas_call | solution.py:311
  40.2 7.0 %all-to-all-start.2 = ((bf16[32,16,512]{2,1,0:T(8,128)(2,1)}), bf16[32,16,512]{2,1,0:T(8,128)(2,1)S(1)}, u32[]{:S(2)}, u32[]{:S(2)}) async-start(bf16[32,16,512]{2,1,0:T(8,128)(2,1)} %bitcast.5), calls=%async_computation.2 | async-start | bytes 1048576 | tf_op jit(solution)/shard_map/all_to_all | solution.py:425
  47.3 9.1 %resp_part.1 = (bf16[1,256,4096]{2,1,0:T(8,128)(2,1)}, bf16[1,256,512]{2,1,0:T(8,128)(2,1)}, bf16[1,256,512]{2,1,0:T(8,128)(2,1)}) custom-call(bf16[1,256,4096]{2,1,0:T(8,128)(2,1)} %q_ref.2, bf16[1,256,4096]{2,1,0:T(8,128)(2,1)} %do_ref.5, bf16[1,256,512]{2,1,0:T(8,128)(2,1)} %kr_ref.3, bf16[1,256,512]{2,1,0:T(8,128)(2,1)} %vr_ref.3, ...), custom_call_target="tpu_custom_call" | custom-call | flops 5368709120 | bytes 8388608 | tf_op jit(solution)/shard_map/resp_part/pallas_call | solution.py:345
  56.4 0.0 all-to-all-done.2.terms_ref
  56.4 0.2 sum_terms.1
  56.6 7.7 %all_to_all.21.blocks_ref = bf16[8,16,512]{2,1,0:T(8,128)(2,1)S(1)} all-to-all(bf16[8,16,512]{2,1,0:T(8,128)(2,1)S(1)} %sum_terms.1), channel_id=1, replica_groups={{80,64,112,96,16,0,48,32},{81,65,113,97,17,1,49,33},{82,66,114,98,18,2,..., dimensions={0} | all-to-all | bytes 262144 | tf_op jit(solution)/shard_map/all_to_all | solution.py:439
  64.3 0.6 join.1
Async XLA Ops:
  11.6 17.9 %all-to-all-start.1 = ((bf16[32,16,512]{2,1,0:T(8,128)(2,1)}), bf16[32,16,512]{2,1,0:T(8,128)(2,1)S(1)}, u32[]{:S(2)}, u32[]{:S(2)}) async-start(bf16[32,16,512]{2,1,0:T(8,128)(2,1)} %select.5), calls=%async_computation.1 | async-start | bytes 1048576 | tf_op jit(solution)/shard_map/all_to_all | solution.py:421
  40.2 16.2 %all-to-all-start.2 = ((bf16[32,16,512]{2,1,0:T(8,128)(2,1)}), bf16[32,16,512]{2,1,0:T(8,128)(2,1)S(1)}, u32[]{:S(2)}, u32[]{:S(2)}) async-start(bf16[32,16,512]{2,1,0:T(8,128)(2,1)} %bitcast.5), calls=%async_computation.2 | async-start | bytes 1048576 | tf_op jit(solution)/shard_map/all_to_all | solution.py:425

commit v6 on v5

--- a/solution.py
+++ b/solution.py
@@ -13,7 +13,7 @@
 GRP = 8
 HEADS = KVH * GRP
 DEAD = 1e30
-LINES = (14, 4, 0, 5, 7, 8, 1, 3, 6, 9, 11, 12, 2, 10, 13, 15)
+LINES = (13, 7, 3, 4, 6, 11, 0, 2, 5, 8, 10, 15, 1, 9, 12, 14)
 FIRST_PLANE = 4
 TOK = 256
 HALF = 128

time: 65.5 us -> 64.7 us (0.988)
  starting transfers between devices: 17 us -> 14.1 us
  waiting for transfers between devices: 1.92 us -> 3.47 us
    all_to_all x1, starting transfers between devices: 9.94 us -> 8.5 us  [per_device(): own = lax.all_to_all(chosen, BOTH, 0, 0, axis_index_groups=groups)]
    all_to_all x1, starting transfers between devices: 7.03 us -> 5.6 us  [per_device(): lax.all_to_all(grad_p.reshape(mates, ROWS, KVW), BOTH, 0, 0, axis_index_g...]
    all_to_all x1, waiting for transfers between devices: 1.92 us -> 3.28 us  [per_device(): own = lax.all_to_all(chosen, BOTH, 0, 0, axis_index_groups=groups)]
  transfers between devices with their start and end apart: 2 -> 2, of which waited for: 1 -> 2; matrix products, arithmetic and copies ran while one was open for 0% -> 0% of each run, Pallas kernels for 22% -> 23%
where the time goes in v6:
time: 64.7 us; the launch traced here: 64.1 us
  Pallas kernels  27.9 us (43%)
  blocking collectives  17.3 us (27%)
  starting transfers between devices  14.1 us (22%)
  waiting for transfers between devices  3.47 us (5%)
  between operations  1.33 us (2%)
    pallas_call x1, Pallas kernels, prompt_part(): pl.pallas_call(prompt_kernel, grid=(KVH,), in_specs=[in_smem(), wide, wid...  10.7 us
    pallas_call x1, Pallas kernels, resp_part(): pl.pallas_call(resp_kernel, grid=(KVH,), in_specs=[wide, wide, narrow, na...  9.15 us
    all_to_all x1, blocking collectives, per_device(): every = lax.all_to_all(spread, 'prompt', 0, 0, axis_index_groups=column)  9.08 us
    all_to_all x1, starting transfers between devices, per_device(): own = lax.all_to_all(chosen, BOTH, 0, 0, axis_index_groups=groups)  8.5 us
    all_to_all x1, blocking collectives, per_device(): owned = lax.all_to_all(sums, 'prompt', 0, 0, axis_index_groups=column)  8.21 us
    all_to_all x1, starting transfers between devices, per_device(): lax.all_to_all(grad_p.reshape(mates, ROWS, KVW), BOTH, 0, 0, axis_index_g...  5.6 us
    pallas_call x1, Pallas kernels, resp_stats(): pl.pallas_call(resp_stats_kernel, grid=(KVH,), in_specs=[wide, wide, narr...  5.42 us
    all_to_all x1, waiting for transfers between devices, per_device(): own = lax.all_to_all(chosen, BOTH, 0, 0, axis_index_groups=groups)  3.28 us
  transfers between devices with their start and end apart: 2, of which 2 were waited for; matrix products, arithmetic and copies ran while one was open for 0% of the time, Pallas kernels for 23%

profile of v6, /device:TPU:1, one launch (start us, length us, event | category | flops | bytes accessed | tf_op | source)
XLA Modules:
  0.0 64.1 jit_solution(3135019215475201103)
XLA Ops:
  0.6 1.1 %prepare.1 = (bf16[8,16,512]{2,1,0:T(8,128)(2,1)S(1)}, s32[32]{0:T(128)S(4)}) custom-call(bf16[1,16,512]{2,1,0:T(8,128)(2,1)} %keys_hbm.1, bf16[1,16,512]{2,1,0:T(8,128)(2,1)} %values_hbm.1, s32[8]{0:T(128)} %sizes_hbm.1, s32[128]{0:T(128)} %slots_hbm.1, s32[1]{0:T(128)} %bitcast.first_ref), custom_call_target="tpu_custom_call" | custom-call | tf_op jit(solution)/shard_map/prepare/pallas_call | solution.py:390
  1.7 9.1 %all_to_all.20.blocks_ref = bf16[8,16,512]{2,1,0:T(8,128)(2,1)S(1)} all-to-all(bf16[8,16,512]{2,1,0:T(8,128)(2,1)S(1)} %get-tuple-element.23), channel_id=1, replica_groups={{80,64,112,96,16,0,48,32},{81,65,113,97,17,1,49,33},{82,66,114,98,18,2,..., dimensions={0} | all-to-all | bytes 262144 | tf_op jit(solution)/shard_map/all_to_all | solution.py:412
  10.8 0.8 %select.5 = bf16[32,16,512]{2,1,0:T(8,128)(2,1)} custom-call(s32[32]{0:T(128)S(4)} %get-tuple-element.22.index_ref, bf16[8,16,512]{2,1,0:T(8,128)(2,1)S(1)} %all_to_all.20.blocks_ref), custom_call_target="tpu_custom_call" | custom-call | tf_op jit(solution)/shard_map/select/pallas_call | solution.py:413
  11.6 8.5 %all-to-all-start.1 = ((bf16[32,16,512]{2,1,0:T(8,128)(2,1)}), bf16[32,16,512]{2,1,0:T(8,128)(2,1)S(1)}, u32[]{:S(2)}, u32[]{:S(2)}) async-start(bf16[32,16,512]{2,1,0:T(8,128)(2,1)} %select.5), calls=%async_computation.1 | async-start | bytes 1048576 | tf_op jit(solution)/shard_map/all_to_all | solution.py:421
  20.8 5.4 %resp_stats.1.stats_ref = f32[32,8,256]{2,1,0:T(8,128)} custom-call(bf16[1,256,4096]{2,1,0:T(8,128)(2,1)} %q_ref.2, bf16[1,256,4096]{2,1,0:T(8,128)(2,1)} %do_ref.5, bf16[1,256,512]{2,1,0:T(8,128)(2,1)} %kr_ref.3, bf16[1,256,512]{2,1,0:T(8,128)(2,1)} %vr_ref.3), custom_call_target="tpu_custom_call" | custom-call | flops 1610612736 | bytes 8388608 | tf_op jit(solution)/shard_map/resp_stats/pallas_call | solution.py:293
  26.2 3.3 %all-to-all-done.1 = bf16[32,16,512]{2,1,0:T(8,128)(2,1)S(1)} async-done(((bf16[32,16,512]{2,1,0:T(8,128)(2,1)}), bf16[32,16,512]{2,1,0:T(8,128)(2,1)S(1)}, u32[]{:S(2)}, u32[]{:S(2)}) %all-to-all-start.1) | async-done | bytes 524320 | tf_op jit(solution)/shard_map/all_to_all | solution.py:421
  29.5 10.7 %prompt_part.1 = (bf16[2,256,512]{2,1,0:T(8,128)(2,1)}, bf16[256,512]{1,0:T(8,128)(2,1)}, bf16[256,8192]{1,0:T(8,128)(2,1)}, f32[32,8,256]{2,1,0:T(8,128)}) custom-call(s32[1]{0:T(128)S(6)} %copy.14.length_ref, bf16[1,256,4096]{2,1,0:T(8,128)(2,1)} %q_ref.2, bf16[1,256,4096]{2,1,0:T(8,128)(2,1)} %do_ref.5, bf16[2,256,512]{2,1,0:T(8,128)(2,1)S(1)} %bitcast.3, ...), custom_call_target="tpu_custom_call" | custom-call | flops 4294967296 | bytes 8388608 | tf_op jit(solution)/shard_map/prompt_part/pallas_call | solution.py:311
  40.1 5.6 %all-to-all-start.2 = ((bf16[32,16,512]{2,1,0:T(8,128)(2,1)}), bf16[32,16,512]{2,1,0:T(8,128)(2,1)S(1)}, u32[]{:S(2)}, u32[]{:S(2)}) async-start(bf16[32,16,512]{2,1,0:T(8,128)(2,1)} %bitcast.5), calls=%async_computation.2 | async-start | bytes 1048576 | tf_op jit(solution)/shard_map/all_to_all | solution.py:425
  45.8 9.1 %resp_part.1 = (bf16[1,256,4096]{2,1,0:T(8,128)(2,1)}, bf16[1,256,512]{2,1,0:T(8,128)(2,1)}, bf16[1,256,512]{2,1,0:T(8,128)(2,1)}) custom-call(bf16[1,256,4096]{2,1,0:T(8,128)(2,1)} %q_ref.2, bf16[1,256,4096]{2,1,0:T(8,128)(2,1)} %do_ref.5, bf16[1,256,512]{2,1,0:T(8,128)(2,1)} %kr_ref.3, bf16[1,256,512]{2,1,0:T(8,128)(2,1)} %vr_ref.3, ...), custom_call_target="tpu_custom_call" | custom-call | flops 5368709120 | bytes 8388608 | tf_op jit(solution)/shard_map/resp_part/pallas_call | solution.py:345
  54.9 0.2 all-to-all-done.2.terms_ref
  55.1 0.2 sum_terms.1
  55.3 8.2 %all_to_all.21.blocks_ref = bf16[8,16,512]{2,1,0:T(8,128)(2,1)S(1)} all-to-all(bf16[8,16,512]{2,1,0:T(8,128)(2,1)S(1)} %sum_terms.1), channel_id=1, replica_groups={{80,64,112,96,16,0,48,32},{81,65,113,97,17,1,49,33},{82,66,114,98,18,2,..., dimensions={0} | all-to-all | bytes 262144 | tf_op jit(solution)/shard_map/all_to_all | solution.py:439
  63.5 0.6 join.1
Async XLA Ops:
  11.6 17.8 %all-to-all-start.1 = ((bf16[32,16,512]{2,1,0:T(8,128)(2,1)}), bf16[32,16,512]{2,1,0:T(8,128)(2,1)S(1)}, u32[]{:S(2)}, u32[]{:S(2)}) async-start(bf16[32,16,512]{2,1,0:T(8,128)(2,1)} %select.5), calls=%async_computation.1 | async-start | bytes 1048576 | tf_op jit(solution)/shard_map/all_to_all | solution.py:421
  40.1 15.0 %all-to-all-start.2 = ((bf16[32,16,512]{2,1,0:T(8,128)(2,1)}), bf16[32,16,512]{2,1,0:T(8,128)(2,1)S(1)}, u32[]{:S(2)}, u32[]{:S(2)}) async-start(bf16[32,16,512]{2,1,0:T(8,128)(2,1)} %bitcast.5), calls=%async_computation.2 | async-start | bytes 1048576 | tf_op jit(solution)/shard_map/all_to_all | solution.py:425

commit v7 on v6

--- a/solution.py
+++ b/solution.py
@@ -239,8 +239,10 @@
     ):
         right = all_rows(right_ref)
         split = PAIRS * LANES
-        out_ref[0, :HALF] = (matmul(left_ref[:HALF], right) * scale).astype(BF16)
-        out_ref[0, HALF:] = (matmul(left_ref[HALF:, split:], right[split:]) * scale).astype(BF16)
+        late = matmul(left_ref[:, split:], right[split:])
+        early = matmul(left_ref[:HALF, :split], right[:split])
+        out_ref[0, :HALF] = ((late[:HALF] + early) * scale).astype(BF16)
+        out_ref[0, HALF:] = (late[HALF:] * scale).astype(BF16)
 
 
 def in_smem():

time: 64.7 us -> 64.7 us (level)
  no operation moved by 1% of the time
where the time goes in v7:
time: 64.7 us; the launch traced here: 64.1 us
  Pallas kernels  28 us (43%)
  blocking collectives  17.3 us (27%)
  starting transfers between devices  14.1 us (22%)
  waiting for transfers between devices  3.48 us (5%)
  between operations  1.33 us (2%)
    pallas_call x1, Pallas kernels, prompt_part(): pl.pallas_call(prompt_kernel, grid=(KVH,), in_specs=[in_smem(), wide, wid...  10.7 us
    pallas_call x1, Pallas kernels, resp_part(): pl.pallas_call(resp_kernel, grid=(KVH,), in_specs=[wide, wide, narrow, na...  9.13 us
    all_to_all x1, blocking collectives, per_device(): every = lax.all_to_all(spread, 'prompt', 0, 0, axis_index_groups=column)  9.08 us
    all_to_all x1, starting transfers between devices, per_device(): own = lax.all_to_all(chosen, BOTH, 0, 0, axis_index_groups=groups)  8.5 us
    all_to_all x1, blocking collectives, per_device(): owned = lax.all_to_all(sums, 'prompt', 0, 0, axis_index_groups=column)  8.17 us
    all_to_all x1, starting transfers between devices, per_device(): lax.all_to_all(grad_p.reshape(mates, ROWS, KVW), BOTH, 0, 0, axis_index_g...  5.6 us
    pallas_call x1, Pallas kernels, resp_stats(): pl.pallas_call(resp_stats_kernel, grid=(KVH,), in_specs=[wide, wide, narr...  5.42 us
    all_to_all x1, waiting for transfers between devices, per_device(): own = lax.all_to_all(chosen, BOTH, 0, 0, axis_index_groups=groups)  3.28 us
  transfers between devices with their start and end apart: 2, of which 2 were waited for; matrix products, arithmetic and copies ran while one was open for 0% of the time, Pallas kernels for 23%

profile of v7, /device:TPU:1, one launch (start us, length us, event | category | flops | bytes accessed | tf_op | source)
XLA Modules:
  0.0 64.1 jit_solution(17452159994569676227)
XLA Ops:
  0.6 1.1 %prepare.1 = (bf16[8,16,512]{2,1,0:T(8,128)(2,1)S(1)}, s32[32]{0:T(128)S(4)}) custom-call(bf16[1,16,512]{2,1,0:T(8,128)(2,1)} %keys_hbm.1, bf16[1,16,512]{2,1,0:T(8,128)(2,1)} %values_hbm.1, s32[8]{0:T(128)} %sizes_hbm.1, s32[128]{0:T(128)} %slots_hbm.1, s32[1]{0:T(128)} %bitcast.first_ref), custom_call_target="tpu_custom_call" | custom-call | tf_op jit(solution)/shard_map/prepare/pallas_call | solution.py:392
  1.7 9.1 %all_to_all.20.blocks_ref = bf16[8,16,512]{2,1,0:T(8,128)(2,1)S(1)} all-to-all(bf16[8,16,512]{2,1,0:T(8,128)(2,1)S(1)} %get-tuple-element.23), channel_id=1, replica_groups={{80,64,112,96,16,0,48,32},{81,65,113,97,17,1,49,33},{82,66,114,98,18,2,..., dimensions={0} | all-to-all | bytes 262144 | tf_op jit(solution)/shard_map/all_to_all | solution.py:414
  10.8 0.8 %select.5 = bf16[32,16,512]{2,1,0:T(8,128)(2,1)} custom-call(s32[32]{0:T(128)S(4)} %get-tuple-element.22.index_ref, bf16[8,16,512]{2,1,0:T(8,128)(2,1)S(1)} %all_to_all.20.blocks_ref), custom_call_target="tpu_custom_call" | custom-call | tf_op jit(solution)/shard_map/select/pallas_call | solution.py:415
  11.6 8.5 %all-to-all-start.1 = ((bf16[32,16,512]{2,1,0:T(8,128)(2,1)}), bf16[32,16,512]{2,1,0:T(8,128)(2,1)S(1)}, u32[]{:S(2)}, u32[]{:S(2)}) async-start(bf16[32,16,512]{2,1,0:T(8,128)(2,1)} %select.5), calls=%async_computation.1 | async-start | bytes 1048576 | tf_op jit(solution)/shard_map/all_to_all | solution.py:423
  20.8 5.4 %resp_stats.1.stats_ref = f32[32,8,256]{2,1,0:T(8,128)} custom-call(bf16[1,256,4096]{2,1,0:T(8,128)(2,1)} %q_ref.2, bf16[1,256,4096]{2,1,0:T(8,128)(2,1)} %do_ref.5, bf16[1,256,512]{2,1,0:T(8,128)(2,1)} %kr_ref.3, bf16[1,256,512]{2,1,0:T(8,128)(2,1)} %vr_ref.3), custom_call_target="tpu_custom_call" | custom-call | flops 1610612736 | bytes 8388608 | tf_op jit(solution)/shard_map/resp_stats/pallas_call | solution.py:295
  26.2 3.3 %all-to-all-done.1 = bf16[32,16,512]{2,1,0:T(8,128)(2,1)S(1)} async-done(((bf16[32,16,512]{2,1,0:T(8,128)(2,1)}), bf16[32,16,512]{2,1,0:T(8,128)(2,1)S(1)}, u32[]{:S(2)}, u32[]{:S(2)}) %all-to-all-start.1) | async-done | bytes 524320 | tf_op jit(solution)/shard_map/all_to_all | solution.py:423
  29.5 10.7 %prompt_part.1 = (bf16[2,256,512]{2,1,0:T(8,128)(2,1)}, bf16[256,512]{1,0:T(8,128)(2,1)}, bf16[256,8192]{1,0:T(8,128)(2,1)}, f32[32,8,256]{2,1,0:T(8,128)}) custom-call(s32[1]{0:T(128)S(6)} %copy.14.length_ref, bf16[1,256,4096]{2,1,0:T(8,128)(2,1)} %q_ref.2, bf16[1,256,4096]{2,1,0:T(8,128)(2,1)} %do_ref.5, bf16[2,256,512]{2,1,0:T(8,128)(2,1)S(1)} %bitcast.3, ...), custom_call_target="tpu_custom_call" | custom-call | flops 4294967296 | bytes 8388608 | tf_op jit(solution)/shard_map/prompt_part/pallas_call | solution.py:313
  40.1 5.6 %all-to-all-start.2 = ((bf16[32,16,512]{2,1,0:T(8,128)(2,1)}), bf16[32,16,512]{2,1,0:T(8,128)(2,1)S(1)}, u32[]{:S(2)}, u32[]{:S(2)}) async-start(bf16[32,16,512]{2,1,0:T(8,128)(2,1)} %bitcast.5), calls=%async_computation.2 | async-start | bytes 1048576 | tf_op jit(solution)/shard_map/all_to_all | solution.py:427
  45.8 9.1 %resp_part.1 = (bf16[1,256,4096]{2,1,0:T(8,128)(2,1)}, bf16[1,256,512]{2,1,0:T(8,128)(2,1)}, bf16[1,256,512]{2,1,0:T(8,128)(2,1)}) custom-call(bf16[1,256,4096]{2,1,0:T(8,128)(2,1)} %q_ref.2, bf16[1,256,4096]{2,1,0:T(8,128)(2,1)} %do_ref.5, bf16[1,256,512]{2,1,0:T(8,128)(2,1)} %kr_ref.3, bf16[1,256,512]{2,1,0:T(8,128)(2,1)} %vr_ref.3, ...), custom_call_target="tpu_custom_call" | custom-call | flops 5368709120 | bytes 8388608 | tf_op jit(solution)/shard_map/resp_part/pallas_call | solution.py:347
  54.9 0.2 all-to-all-done.2.terms_ref
  55.1 0.2 sum_terms.1
  55.3 8.2 %all_to_all.21.blocks_ref = bf16[8,16,512]{2,1,0:T(8,128)(2,1)S(1)} all-to-all(bf16[8,16,512]{2,1,0:T(8,128)(2,1)S(1)} %sum_terms.1), channel_id=1, replica_groups={{80,64,112,96,16,0,48,32},{81,65,113,97,17,1,49,33},{82,66,114,98,18,2,..., dimensions={0} | all-to-all | bytes 262144 | tf_op jit(solution)/shard_map/all_to_all | solution.py:441
  63.5 0.6 join.1
Async XLA Ops:
  11.6 17.8 %all-to-all-start.1 = ((bf16[32,16,512]{2,1,0:T(8,128)(2,1)}), bf16[32,16,512]{2,1,0:T(8,128)(2,1)S(1)}, u32[]{:S(2)}, u32[]{:S(2)}) async-start(bf16[32,16,512]{2,1,0:T(8,128)(2,1)} %select.5), calls=%async_computation.1 | async-start | bytes 1048576 | tf_op jit(solution)/shard_map/all_to_all | solution.py:423
  40.1 15.0 %all-to-all-start.2 = ((bf16[32,16,512]{2,1,0:T(8,128)(2,1)}), bf16[32,16,512]{2,1,0:T(8,128)(2,1)S(1)}, u32[]{:S(2)}, u32[]{:S(2)}) async-start(bf16[32,16,512]{2,1,0:T(8,128)(2,1)} %bitcast.5), calls=%async_computation.2 | async-start | bytes 1048576 | tf_op jit(solution)/shard_map/all_to_all | solution.py:427
